TPU v7x, 256 devices: a whole 4x4x8 slice. The times are simulated.
256 devices in a mesh: req: 4 (over x), cand: 64 (over y, z, core).
Axes of the slice: x: 4, y: 4, z: 8, core: 2. Of those that a mesh axis runs over, the one named last changes fastest.
Arguments:
- cand_emb: bfloat16 [131072, 512], P(('req', 'cand')), may hold values from -6 to 6
- cand_req: int32 [131072], P(('req', 'cand')), may hold values from 0 to 31, as said below
- expert_ids: int32 [131072], P(('req', 'cand')), may hold values from 0 to 63, as said below
- user_state: bfloat16 [1024, 512], P(('req', 'cand')), may hold values from -6 to 6
- d_out: bfloat16 [131072, 512], P(('req', 'cand')), may hold values from -6 to 6
- w_in: bfloat16 [64, 512, 2048], P('cand'), may hold values from -0.25 to 0.25
- w_out: bfloat16 [64, 2048, 512], P('cand'), may hold values from -0.125 to 0.125
Outputs:
- tower_out: bfloat16 [131072, 512], P(('req', 'cand'))
- cand_grad: bfloat16 [131072, 512], P(('req', 'cand'))
- user_grad: float32 [1024, 512], P(('req', 'cand'))
Inputs may be any that keep to these rules, and one draw needn't show every extreme that they name: `cand_req`: candidates on devices with req index g name requests g * 8 to g * 8 + 7. `expert_ids`: in each device's aligned block of 512 rows no expert is named by more than 16 rows; on the devices of one req index one expert is named exactly 16 times in every block.
All inputs are finite; a program needn't handle non-finite values.
Results may differ from a plain program's by a relative error of at most 0.0076.
Values may be sent and summed in bfloat16 or wider, within the bound.
No kernel may reach another device: no remote copies, remote signals or barrier semaphores. Data moves between devices by JAX's collectives and lax.ppermute only.
A program may use at most 64 MiB of HBM per device.

v0:
```python
from functools import partial
import math

import jax
import jax.numpy as jnp
from jax import lax
from jax.sharding import PartitionSpec as P

D = 512
US = 32
REQ_DEV = 8


def attend(queries, keys, local_req):
    scale = 1.0 / math.sqrt(D)
    scores = jnp.dot(queries, keys.T, preferred_element_type=jnp.float32) * scale
    member = local_req[:, None] == (jnp.arange(keys.shape[0], dtype=jnp.int32) // US)[None, :]
    peak = jnp.max(jnp.where(member, scores, -jnp.inf), axis=1, keepdims=True)
    weights = jnp.exp(jnp.where(member, scores - peak, -jnp.inf))
    return weights / jnp.sum(weights, axis=1, keepdims=True)


def expert_rows(piece, w_in, w_out, forward, backward):
    local_experts, sources, slots, payload = piece.shape
    width = w_in.shape[1]
    flat = piece.reshape(local_experts, sources * slots, payload)
    inputs = flat[:, :, :width]
    pre = jnp.einsum("erd,edf->erf", inputs, w_in, preferred_element_type=jnp.float32)
    results = []
    if forward:
        hidden = jax.nn.gelu(pre).astype(jnp.bfloat16)
        results.append(
            jnp.einsum("erf,efd->erd", hidden, w_out, preferred_element_type=jnp.float32).astype(
                jnp.bfloat16
            )
        )
    if backward:
        grads = flat[:, :, width:]
        back = jnp.einsum("erd,efd->erf", grads, w_out, preferred_element_type=jnp.float32)
        activated, pull_back = jax.vjp(jax.nn.gelu, pre)
        d_pre = pull_back(back)[0].astype(jnp.bfloat16)
        results.append(
            jnp.einsum("erf,edf->erd", d_pre, w_in, preferred_element_type=jnp.float32).astype(
                jnp.bfloat16
            )
        )
    joined = results[0].reshape(local_experts, sources, slots, -1)
    return lax.all_to_all(joined, "cand", split_axis=1, concat_axis=0, tiled=True)


def expert_trip(payload, w_in, w_out, forward, backward):
    worker = partial(expert_rows, w_in=w_in, w_out=w_out, forward=forward, backward=backward)
    return worker(lax.all_to_all(payload, "cand", split_axis=0, concat_axis=1, tiled=True))


def shards(cand_emb, cand_req, expert_ids, user_state, d_out, w_in, w_out):
    row_count, width = cand_emb.shape
    scale = 1.0 / math.sqrt(width)
    experts = lax.axis_size("cand") * w_in.shape[0]
    capacity = 2 * row_count // experts
    group_keys = lax.all_gather(user_state, "cand", axis=0, tiled=True)
    local_req = cand_req - lax.axis_index("req") * REQ_DEV
    probs = attend(cand_emb, group_keys, local_req)
    probs_b = probs.astype(jnp.bfloat16)
    mixed = jnp.dot(probs_b, group_keys, preferred_element_type=jnp.float32)
    tower_in = (cand_emb.astype(jnp.float32) + mixed).astype(jnp.bfloat16)
    onehot = (expert_ids[:, None] == jnp.arange(experts, dtype=jnp.int32)[None, :]).astype(
        jnp.int32
    )
    ranks = jnp.cumsum(onehot, axis=0) - 1
    slot = jnp.sum(onehot * ranks, axis=1)

    def pack(values):
        empty = jnp.zeros((experts, 1, capacity, values.shape[1]), jnp.bfloat16)
        return empty.at[expert_ids, 0, slot].set(values)

    def unpack(back):
        return back[expert_ids, 0, slot]

    tower_out = unpack(expert_trip(pack(tower_in), w_in, w_out, True, False))
    d_in = unpack(
        expert_trip(pack(jnp.concatenate([tower_in, d_out], axis=1)), w_in, w_out, False, True)
    )
    d_probs = jnp.dot(d_in, group_keys.T, preferred_element_type=jnp.float32)
    center = jnp.sum(probs * d_probs, axis=1, keepdims=True)
    slope = (probs * (d_probs - center)).astype(jnp.bfloat16)
    cand_grad = (
        d_in.astype(jnp.float32)
        + jnp.dot(slope, group_keys, preferred_element_type=jnp.float32) * scale
    ).astype(jnp.bfloat16)
    term = jnp.dot(probs_b.T, d_in, preferred_element_type=jnp.float32)
    user_grad = lax.psum_scatter(
        term + jnp.dot(slope.T, cand_emb, preferred_element_type=jnp.float32) * scale,
        "cand",
        scatter_dimension=0,
        tiled=True,
    )
    return (tower_out, cand_grad, user_grad)


def solution(mesh):
    in_specs = (
        P(("req", "cand"), None),
        P(("req", "cand")),
        P(("req", "cand")),
        P(("req", "cand"), None),
        P(("req", "cand"), None),
        P("cand", None, None),
        P("cand", None, None),
    )
    out_specs = (P(("req", "cand"), None), P(("req", "cand"), None), P(("req", "cand"), None))
    return jax.shard_map(shards, mesh=mesh, in_specs=in_specs, out_specs=out_specs, check_vma=False)
```

profile of v0, /device:TPU:1, one launch (start us, length us, event | category | flops | bytes accessed | tf_op | source)
XLA Modules:
  0.0 542.5 jit_solution(17772102423287951227)
XLA Ops:
  7.2 0.0 copy-start
  7.2 0.8 clamp_shift-left_fusion.2
  8.0 0.7 fusion.57
  8.7 1.2 reduce-window.6
  9.9 0.2 slice_reduce_fusion
  10.2 0.8 fusion.53
  11.0 48.9 %all-gather = bf16[64,4,512]{2,1,0:T(4,128)(2,1)S(1)} all-gather(bf16[1,4,512]{2,1,0:T(4,128)(2,1)} %bitcast.89), channel_id=1, replica_groups=mesh['req'=4,'cand'=64] {'cand'}, dimensions={0}, use_global_device_ids=true | all-gather | bytes 266240 | tf_op jit(solution)/shard_map/all_gather | solution.py:61
  59.9 0.1 reshape.187
  60.0 0.0 copy-start.3
  60.0 2.1 copy.18
  62.1 0.7 broadcast_subtract_fusion
  62.8 1.4 fusion.48
  64.2 0.0 copy-start.2
  64.2 0.2 fusion.51
  64.4 0.0 copy-done.3
  64.4 0.6 copy-done.2
  65.0 1.5 fusion.45
  66.5 0.2 copy.19
  66.8 1.1 broadcast.197
  67.9 64.2 %scatter_fusion = bf16[64,16,512]{2,1,0:T(8,128)(2,1)} fusion(bf16[64,16,512]{2,1,0:T(8,128)(2,1)} %broadcast.197, s32[512]{0:T(512)S(1)} %bitcast.77, bf16[512,512]{1,0:T(8,128)(2,1)S(1)} %copy.19), kind=kCustom, calls=%fused_computation.2 | custom fusion | bytes 1576960 | tf_op jit(solution)/shard_map/scatter | solution.py:75
  132.1 6.6 %all-to-all-start = ((bf16[64,1,16,512]{3,2,1,0:T(8,128)(2,1)}), bf16[64,1,16,512]{3,2,1,0:T(8,128)(2,1)}, u32[]{:S(2)}, u32[]{:S(2)}) async-start(bf16[64,1,16,512]{3,2,1,0:T(8,128)(2,1)} %bitcast.7), calls=%async_computation | async-start | bytes 2097152 | tf_op jit(solution)/shard_map/all_to_all | solution.py:53
  138.7 1.3 copy.22
  140.0 1.1 pad_maximum_fusion
  141.1 1.5 copy.23
  142.5 1.6 broadcast.209
  144.2 71.6 %scatter_fusion.1 = bf16[64,16,1024]{2,1,0:T(8,128)(2,1)} fusion(bf16[64,16,1024]{2,1,0:T(8,128)(2,1)} %broadcast.209, s32[512]{0:T(512)S(1)} %bitcast.78, bf16[512,1024]{1,0:T(8,128)(2,1)S(1)} %copy.23), kind=kCustom, calls=%fused_computation.3 | custom fusion | bytes 3149824 | tf_op jit(solution)/shard_map/scatter | solution.py:75
  215.8 0.0 all-to-all-done
  215.8 10.6 %all-to-all-start.2 = ((bf16[64,1,16,1024]{3,2,1,0:T(8,128)(2,1)}), bf16[64,1,16,1024]{3,2,1,0:T(8,128)(2,1)}, u32[]{:S(2)}, u32[]{:S(2)}) async-start(bf16[64,1,16,1024]{3,2,1,0:T(8,128)(2,1)} %bitcast.81), calls=%async_computation.2 | async-start | bytes 4194304 | tf_op jit(solution)/shard_map/all_to_all | solution.py:53
  226.4 0.0 copy-done
  226.4 7.7 %fusion.37 = bf16[1024,512]{1,0:T(8,128)(2,1)} fusion(bf16[1,2048,512]{2,1,0:T(8,128)(2,1)S(1)} %copy-done, bf16[1024,512]{1,0:T(8,128)(2,1)} %bitcast.8, bf16[1,512,2048]{2,1,0:T(8,128)(2,1)} %param.12), kind=kOutput, calls=%fused_computation.32 | convolution fusion | flops 4314365952 | bytes 6291456 | tf_op jit(solution)/shard_map/erf,efd->erd/dot_general | solution.py:33
  234.1 43.5 %all-to-all-done.2 = bf16[64,1,16,1024]{3,2,1,0:T(8,128)(2,1)} async-done(((bf16[64,1,16,1024]{3,2,1,0:T(8,128)(2,1)}), bf16[64,1,16,1024]{3,2,1,0:T(8,128)(2,1)}, u32[]{:S(2)}, u32[]{:S(2)}) %all-to-all-start.2) | async-done | bytes 2097184 | tf_op jit(solution)/shard_map/all_to_all | solution.py:53
  277.6 5.8 %all-to-all-start.1 = ((bf16[1,64,16,512]{3,2,0,1:T(8,128)(2,1)}), bf16[1,64,16,512]{3,2,0,1:T(8,128)(2,1)S(1)}, u32[]{:S(2)}, u32[]{:S(2)}) async-start(bf16[1,64,16,512]{3,2,0,1:T(8,128)(2,1)} %bitcast.84), calls=%async_computation.1 | async-start | bytes 2097152 | tf_op jit(solution)/shard_map/all_to_all | solution.py:48
  283.4 6.8 %fusion.21 = f32[1024,2048]{1,0:T(8,128)} fusion(bf16[1,2048,512]{2,1,0:T(8,128)(2,1)S(1)} %copy-done, bf16[1,1024,1024]{2,1,0:T(8,128)(2,1)} %bitcast.18), kind=kOutput, calls=%fused_computation.25 | convolution fusion | flops 2147483648 | bytes 11534336 | tf_op jit(solution)/shard_map/erd,efd->erf/dot_general | solution.py:39
  290.2 0.0 copy-start.4
  290.2 12.9 %fusion.30 = bf16[1024,512]{1,0:T(8,128)(2,1)} fusion(bf16[1,512,2048]{2,1,0:T(8,128)(2,1)} %param.12, f32[1024,2048]{1,0:T(8,128)} %fusion.21, bf16[1,1024,1024]{2,1,0:T(8,128)(2,1)} %bitcast.18), kind=kOutput, calls=%fused_computation.31 | convolution fusion | flops 4337434624 | bytes 14680064 | tf_op jit(solution)/shard_map/erf,edf->erd/dot_general | solution.py:43
  303.1 8.8 %all-to-all-done.1 = bf16[1,64,16,512]{3,2,0,1:T(8,128)(2,1)S(1)} async-done(((bf16[1,64,16,512]{3,2,0,1:T(8,128)(2,1)}), bf16[1,64,16,512]{3,2,0,1:T(8,128)(2,1)S(1)}, u32[]{:S(2)}, u32[]{:S(2)}) %all-to-all-start.1) | async-done | bytes 1048608 | tf_op jit(solution)/shard_map/all_to_all | solution.py:48
  312.0 6.4 %all-to-all-start.3 = ((bf16[1,64,16,512]{3,2,0,1:T(8,128)(2,1)}), bf16[1,64,16,512]{3,2,0,1:T(8,128)(2,1)}, u32[]{:S(2)}, u32[]{:S(2)}) async-start(bf16[1,64,16,512]{3,2,0,1:T(8,128)(2,1)} %bitcast.83), calls=%async_computation.3 | async-start | bytes 2097152 | tf_op jit(solution)/shard_map/all_to_all | solution.py:48
  318.3 0.3 all-reduce.3.cloned.1.call-start
  318.7 0.0 copy-done.4
  318.7 0.6 dynamic-slice
  319.9 5.2 gather_fusion
  325.1 0.0 copy-start.1
  325.1 21.7 %all-to-all-done.3 = bf16[1,64,16,512]{3,2,0,1:T(8,128)(2,1)} async-done(((bf16[1,64,16,512]{3,2,0,1:T(8,128)(2,1)}), bf16[1,64,16,512]{3,2,0,1:T(8,128)(2,1)}, u32[]{:S(2)}, u32[]{:S(2)}) %all-to-all-start.3) | async-done | bytes 1048608 | tf_op jit(solution)/shard_map/all_to_all | solution.py:48
  346.8 5.5 %gather_fusion.1 = bf16[512,512]{1,0:T(8,128)(2,1)S(1)} fusion(bf16[64,1,16,512]{3,2,1,0:T(8,128)(2,1)} %bitcast.23, s32[512]{0:T(512)S(1)} %bitcast.80), kind=kCustom, calls=%fused_computation.1 | custom fusion | bytes 1054720 | tf_op jit(solution)/shard_map/gather | solution.py:78
  352.3 1.5 multiply_reduce_fusion
  353.8 1.4 fusion.54
  355.3 1.3 multiply_convert_fusion
  356.5 0.0 copy-done.1
  356.5 1.1 fusion.47
  357.7 0.0 all-reduce.3.cloned.1.call-update
  357.7 2.1 fusion.46
  359.8 174.6 %all-reduce.3.cloned.1.call-done = f32[256,512]{1,0:T(8,128)} async-done(((f32[256,512]{1,0:T(8,128)}), f32[256,512]{1,0:T(8,128)}) %all-reduce.3.cloned.1.call-update) | async-done | bytes 524304
  534.3 1.3 constant_dynamic-slice_fusion
  (4 shorter events, 0.1 us)
Async XLA Ops:
  7.2 219.3 %copy-start = (bf16[1,2048,512]{2,1,0:T(8,128)(2,1)S(1)}, bf16[1,2048,512]{2,1,0:T(8,128)(2,1)}, u32[]{:S(2)}) copy-start(bf16[1,2048,512]{2,1,0:T(8,128)(2,1)} %param.13) | copy-start | bytes 6291460
  60.0 4.4 copy-start.3
  64.2 0.8 copy-start.2
  132.1 83.7 %all-to-all-start = ((bf16[64,1,16,512]{3,2,1,0:T(8,128)(2,1)}), bf16[64,1,16,512]{3,2,1,0:T(8,128)(2,1)}, u32[]{:S(2)}, u32[]{:S(2)}) async-start(bf16[64,1,16,512]{3,2,1,0:T(8,128)(2,1)} %bitcast.7), calls=%async_computation | async-start | bytes 2097152 | tf_op jit(solution)/shard_map/all_to_all | solution.py:53
  215.8 61.8 %all-to-all-start.2 = ((bf16[64,1,16,1024]{3,2,1,0:T(8,128)(2,1)}), bf16[64,1,16,1024]{3,2,1,0:T(8,128)(2,1)}, u32[]{:S(2)}, u32[]{:S(2)}) async-start(bf16[64,1,16,1024]{3,2,1,0:T(8,128)(2,1)} %bitcast.81), calls=%async_computation.2 | async-start | bytes 4194304 | tf_op jit(solution)/shard_map/all_to_all | solution.py:53
  277.6 34.4 %all-to-all-start.1 = ((bf16[1,64,16,512]{3,2,0,1:T(8,128)(2,1)}), bf16[1,64,16,512]{3,2,0,1:T(8,128)(2,1)S(1)}, u32[]{:S(2)}, u32[]{:S(2)}) async-start(bf16[1,64,16,512]{3,2,0,1:T(8,128)(2,1)} %bitcast.84), calls=%async_computation.1 | async-start | bytes 2097152 | tf_op jit(solution)/shard_map/all_to_all | solution.py:48
  290.2 28.4 %copy-start.4 = (u32[256]{0:T(256)S(1)}, u32[256]{0:T(256)}, u32[]{:S(2)}) copy-start(u32[256]{0:T(256)} %constant.149) | copy-start | bytes 3076
  312.0 34.9 %all-to-all-start.3 = ((bf16[1,64,16,512]{3,2,0,1:T(8,128)(2,1)}), bf16[1,64,16,512]{3,2,0,1:T(8,128)(2,1)}, u32[]{:S(2)}, u32[]{:S(2)}) async-start(bf16[1,64,16,512]{3,2,0,1:T(8,128)(2,1)} %bitcast.83), calls=%async_computation.3 | async-start | bytes 2097152 | tf_op jit(solution)/shard_map/all_to_all | solution.py:48
  318.3 216.0 %all-reduce.3.cloned.1.call-start = ((), (), s32[]{:S(2)}) async-start(), calls=%async_computation.4 | async-start | bytes 1048576
  325.1 31.5 %copy-start.1 = (bf16[512,512]{1,0:T(8,128)(2,1)S(1)}, bf16[512,512]{1,0:T(8,128)(2,1)}, u32[]{:S(2)}) copy-start(bf16[512,512]{1,0:T(8,128)(2,1)} %param.7) | copy-start | bytes 1572868
Sparse Core Ops, SparseCore 0:
  357.8 176.4 all-reduce.2
where the time goes:
time: 549 us; the launch traced here: 542 us
  waiting for transfers between devices  249 us (45%)
  local copies, waits for them, and re-layouts  157 us (29%)
  blocking collectives  48.9 us (9%)
  matrix products  36.4 us (7%)
  starting transfers between devices  29.7 us (5%)
  between operations  14.9 us (3%)
  other arithmetic  6.78 us (1%)
    unnamed x2, waiting for transfers between devices  175 us
    scatter x2, local copies, waits for them, and re-layouts, pack(): return empty.at[expert_ids, 0, slot].set(values)  136 us
    all_gather x1, blocking collectives, shards(): group_keys = lax.all_gather(user_state, 'cand', axis=0, tiled=True)  48.9 us
    all_to_all x2, waiting for transfers between devices, expert_trip(): lax.all_to_all(payload, 'cand', split_axis=0, concat_axis=1, tiled=True)  43.5 us
    all_to_all x2, waiting for transfers between devices, expert_rows(): lax.all_to_all(joined, 'cand', split_axis=1, concat_axis=0, tiled=True)  30.6 us
    all_to_all x2, starting transfers between devices, expert_trip(): lax.all_to_all(payload, 'cand', split_axis=0, concat_axis=1, tiled=True)  17.2 us
    dot_general x1, matrix products, expert_rows(): jnp.einsum('erf,edf->erd', d_pre, w_in, preferred_element_type=jnp.float32)  12.9 us
    all_to_all x2, starting transfers between devices, expert_rows(): lax.all_to_all(joined, 'cand', split_axis=1, concat_axis=0, tiled=True)  12.2 us
  transfers between devices with their start and end apart: 5, of which 4 were waited for; matrix products, arithmetic and copies ran while one was open for 21% of the time, Pallas kernels for 0%

commit v1 on v0

v1 whole, which is shorter than its diff:
```python
import math

import jax
import jax.numpy as jnp
from jax import lax
from jax.sharding import PartitionSpec as P

US = 32
REQ_DEV = 8


def dot(a, b, dims):
    return lax.dot_general(a, b, (dims, ((), ())), preferred_element_type=jnp.float32)


def exchange(blocks):
    return lax.all_to_all(blocks, "cand", split_axis=0, concat_axis=0, tiled=True)


def shards(cand_emb, cand_req, expert_ids, user_state, d_out, w_in, w_out):
    row_count, width = cand_emb.shape
    scale = 1.0 / math.sqrt(width)
    devices = lax.axis_size("cand")
    experts = devices * w_in.shape[0]
    capacity = 2 * row_count // experts
    slots = experts * capacity
    w_in, w_out = w_in[0], w_out[0]

    keys = exchange(jnp.broadcast_to(user_state[None], (devices,) + user_state.shape))
    keys = keys.reshape(-1, width)

    onehot = (expert_ids[:, None] == jnp.arange(experts, dtype=jnp.int32)[None, :]).astype(jnp.bfloat16)
    rows = jnp.arange(row_count, dtype=jnp.int32)
    below = (rows[:, None] > rows[None, :]).astype(jnp.bfloat16)
    ranks = dot(below, onehot, ((1,), (0,)))
    slot = jnp.sum(onehot.astype(jnp.float32) * ranks, axis=1).astype(jnp.int32)
    place = expert_ids * capacity + slot
    spread = (jnp.arange(slots, dtype=jnp.int32)[:, None] == place[None, :]).astype(jnp.bfloat16)

    def send(values):
        packed = dot(spread, values, ((1,), (0,))).astype(jnp.bfloat16)
        return exchange(packed.reshape(devices, capacity, width)).reshape(slots, width)

    def fetch(values):
        back = exchange(values.reshape(devices, capacity, width)).reshape(slots, width)
        return dot(spread, back, ((0,), (0,))).astype(jnp.bfloat16)

    grads = send(d_out)

    local_req = cand_req - lax.axis_index("req") * REQ_DEV
    scores = dot(cand_emb, keys, ((1,), (1,))) * scale
    member = local_req[:, None] == (jnp.arange(keys.shape[0], dtype=jnp.int32) // US)[None, :]
    peak = jnp.max(jnp.where(member, scores, -jnp.inf), axis=1, keepdims=True)
    weights = jnp.exp(jnp.where(member, scores - peak, -jnp.inf))
    probs = weights / jnp.sum(weights, axis=1, keepdims=True)
    probs_b = probs.astype(jnp.bfloat16)
    tower_in = (cand_emb.astype(jnp.float32) + dot(probs_b, keys, ((1,), (0,)))).astype(jnp.bfloat16)
    inputs = send(tower_in)

    back = dot(grads, w_out, ((1,), (1,)))
    pre = dot(inputs, w_in, ((1,), (0,)))
    activated, pull_back = jax.vjp(jax.nn.gelu, pre)
    d_pre = pull_back(back)[0].astype(jnp.bfloat16)
    d_in = fetch(dot(d_pre, w_in, ((1,), (1,))).astype(jnp.bfloat16))
    hidden = activated.astype(jnp.bfloat16)
    tower_out = fetch(dot(hidden, w_out, ((1,), (0,))).astype(jnp.bfloat16))

    d_probs = dot(d_in, keys, ((1,), (1,)))
    center = jnp.sum(probs * d_probs, axis=1, keepdims=True)
    slope = (probs * (d_probs - center)).astype(jnp.bfloat16)
    share = dot(probs_b, d_in, ((0,), (0,))) + dot(slope, cand_emb, ((0,), (0,))) * scale
    shares = exchange(share.astype(jnp.bfloat16).reshape(devices, -1, width))
    user_grad = jnp.sum(shares.astype(jnp.float32), axis=0)
    cand_grad = (d_in.astype(jnp.float32) + dot(slope, keys, ((1,), (0,))) * scale).astype(jnp.bfloat16)
    return (tower_out, cand_grad, user_grad)


def solution(mesh):
    rows = P(("req", "cand"), None)
    ids = P(("req", "cand"))
    weights = P("cand", None, None)
    in_specs = (rows, ids, ids, rows, rows, weights, weights)
    return jax.shard_map(shards, mesh=mesh, in_specs=in_specs, out_specs=(rows, rows, rows), check_vma=False)
```

time: 549 us -> 204 us (0.37)
  local copies, waits for them, and re-layouts: 157 us -> 2.46 us
  waiting for transfers between devices: 249 us -> 109 us
  blocking collectives: 48.9 us -> 0 us
  starting transfers between devices: 29.7 us -> 44.7 us
  between operations: 14.9 us -> 0.77 us
  matrix products: 36.4 us -> 44.3 us
    unnamed x2 -> x0, waiting for transfers between devices: 175 us -> none
    scatter x2 -> x0, local copies, waits for them, and re-layouts: 136 us -> none  [pack(): return empty.at[expert_ids, 0, slot].set(values)]
    all_gather x1 -> x0, blocking collectives: 48.9 us -> none  [shards(): group_keys = lax.all_gather(user_state, 'cand', axis=0, tiled=True)]
    all_to_all x4 -> x6, waiting for transfers between devices: 74 us -> 109 us  [exchange(): lax.all_to_all(blocks, 'cand', split_axis=0, concat_axis=0, tiled=True)]
    all_to_all x4 -> x6, starting transfers between devices: 29.4 us -> 44.7 us  [exchange(): lax.all_to_all(blocks, 'cand', split_axis=0, concat_axis=0, tiled=True)]
    gather x2 -> x0, local copies, waits for them, and re-layouts: 10.7 us -> none  [unpack(): return back[expert_ids, 0, slot]]
    dot_general x9 -> x13, matrix products: 36.4 us -> 44.3 us  [dot(): lax.dot_general(a, b, (dims, ((), ())), preferred_element_type=jnp.float32)]
    unnamed x15 -> x4, local copies, waits for them, and re-layouts: 6.01 us -> 0.02 us
  transfers between devices with their start and end apart: 5 -> 6, of which waited for: 4 -> 6; matrix products, arithmetic and copies ran while one was open for 21% -> 14% of each run, Pallas kernels for 0% -> 0%
where the time goes in v1:
time: 204 us; the launch traced here: 203 us
  waiting for transfers between devices  109 us (53%)
  starting transfers between devices  44.7 us (22%)
  matrix products  44.3 us (22%)
  local copies, waits for them, and re-layouts  2.46 us (1%)
    all_to_all x6, waiting for transfers between devices, exchange(): lax.all_to_all(blocks, 'cand', split_axis=0, concat_axis=0, tiled=True)  109 us
    all_to_all x6, starting transfers between devices, exchange(): lax.all_to_all(blocks, 'cand', split_axis=0, concat_axis=0, tiled=True)  44.7 us
    dot_general x13, matrix products, dot(): lax.dot_general(a, b, (dims, ((), ())), preferred_element_type=jnp.float32)  44.3 us
  transfers between devices with their start and end apart: 6, of which 6 were waited for; matrix products, arithmetic and copies ran while one was open for 14% of the time, Pallas kernels for 0%

profile of v1, /device:TPU:1, one launch (start us, length us, event | category | flops | bytes accessed | tf_op | source)
XLA Modules:
  0.0 202.9 jit_solution(363848814458069854)
XLA Ops:
  0.6 0.0 copy-start
  0.6 1.6 broadcast_in_dim.6
  2.3 13.2 %all-to-all-start = ((bf16[64,4,512]{2,1,0:T(4,128)(2,1)}), bf16[64,4,512]{2,1,0:T(4,128)(2,1)S(1)}, u32[]{:S(2)}, u32[]{:S(2)}) async-start(bf16[64,4,512]{2,1,0:T(4,128)(2,1)} %broadcast_in_dim.6), calls=%async_computation | async-start | bytes 524288 | tf_op jit(solution)/shard_map/all_to_all | solution.py:17
  15.4 1.0 fusion.41
  16.5 0.7 convert_add_fusion
  17.2 10.2 %all-to-all-done = bf16[64,4,512]{2,1,0:T(4,128)(2,1)S(1)} async-done(((bf16[64,4,512]{2,1,0:T(4,128)(2,1)}), bf16[64,4,512]{2,1,0:T(4,128)(2,1)S(1)}, u32[]{:S(2)}, u32[]{:S(2)}) %all-to-all-start) | async-done | bytes 262176 | tf_op jit(solution)/shard_map/all_to_all | solution.py:17
  27.4 0.1 reshape.56
  27.5 1.4 fusion.47
  28.9 0.2 fusion.50
  29.1 3.1 %fusion.29 = bf16[1024,512]{1,0:T(8,128)(2,1)} fusion(bf16[256,512]{1,0:T(8,128)(2,1)S(1)} %reshape.56, bf16[512,512]{1,0:T(8,128)(2,1)} %param.7, s32[512]{0:T(512)S(1)} %get-tuple-element.7, f32[512,256]{0,1:T(8,128)S(1)} %get-tuple-element.4, f32[512]{0:T(512)S(1)} %fusion.50, f32[512]{0:T(512)S(1)} %get-tuple-element.3, s32[512]{0:T(512)S(1)} %get-tuple-element.8, ...), kind=kOutput, calls=%fused_computation.24 | convolution fusion | flops 673579008 | bytes 2368512 | tf_op jit(solution)/shard_map/dot_general | solution.py:13
  32.2 6.2 %all-to-all-start.1 = ((bf16[64,16,512]{2,1,0:T(8,128)(2,1)}), bf16[64,16,512]{2,1,0:T(8,128)(2,1)}, u32[]{:S(2)}, u32[]{:S(2)}) async-start(bf16[64,16,512]{2,1,0:T(8,128)(2,1)} %bitcast.43), calls=%async_computation.1 | async-start | bytes 2097152 | tf_op jit(solution)/shard_map/all_to_all | solution.py:17
  38.4 2.7 %fusion.30 = bf16[1024,512]{1,0:T(8,128)(2,1)} fusion(bf16[512,512]{1,0:T(8,128)(2,1)} %param.11, s32[512]{0:T(512)S(1)} %get-tuple-element.7), kind=kOutput, calls=%fused_computation.25 | convolution fusion | flops 537919488 | bytes 1574912 | tf_op jit(solution)/shard_map/dot_general | solution.py:13
  41.1 25.7 %all-to-all-done.1 = bf16[64,16,512]{2,1,0:T(8,128)(2,1)} async-done(((bf16[64,16,512]{2,1,0:T(8,128)(2,1)}), bf16[64,16,512]{2,1,0:T(8,128)(2,1)}, u32[]{:S(2)}, u32[]{:S(2)}) %all-to-all-start.1) | async-done | bytes 1048608 | tf_op jit(solution)/shard_map/all_to_all | solution.py:17
  66.9 6.4 %all-to-all-start.3 = ((bf16[64,16,512]{2,1,0:T(8,128)(2,1)}), bf16[64,16,512]{2,1,0:T(8,128)(2,1)}, u32[]{:S(2)}, u32[]{:S(2)}) async-start(bf16[64,16,512]{2,1,0:T(8,128)(2,1)} %bitcast.41), calls=%async_computation.3 | async-start | bytes 2097152 | tf_op jit(solution)/shard_map/all_to_all | solution.py:17
  73.3 0.0 copy-done
  73.3 6.8 %fusion.16 = f32[1024,2048]{1,0:T(8,128)} fusion(bf16[1024,512]{1,0:T(8,128)(2,1)} %bitcast.1, bf16[1,512,2048]{2,1,0:T(8,128)(2,1)S(1)} %copy-done), kind=kOutput, calls=%fused_computation.16 | convolution fusion | flops 2147483648 | bytes 11534336 | tf_op jit(solution)/shard_map/dot_general | solution.py:13
  80.1 21.7 %all-to-all-done.3 = bf16[64,16,512]{2,1,0:T(8,128)(2,1)} async-done(((bf16[64,16,512]{2,1,0:T(8,128)(2,1)}), bf16[64,16,512]{2,1,0:T(8,128)(2,1)}, u32[]{:S(2)}, u32[]{:S(2)}) %all-to-all-start.3) | async-done | bytes 1048608 | tf_op jit(solution)/shard_map/all_to_all | solution.py:17
  101.7 12.5 %fusion.22 = bf16[1024,512]{1,0:T(8,128)(2,1)} fusion(bf16[1,512,2048]{2,1,0:T(8,128)(2,1)S(1)} %copy-done, f32[1024,2048]{1,0:T(8,128)} %fusion.16, bf16[1024,512]{1,0:T(8,128)(2,1)} %bitcast.7, bf16[1,2048,512]{2,1,0:T(8,128)(2,1)} %param.13), kind=kOutput, calls=%fused_computation.23 | convolution fusion | flops 4337434624 | bytes 14680064 | tf_op jit(solution)/shard_map/dot_general | solution.py:13
  114.2 6.4 %all-to-all-start.4 = ((bf16[64,16,512]{2,1,0:T(8,128)(2,1)}), bf16[64,16,512]{2,1,0:T(8,128)(2,1)}, u32[]{:S(2)}, u32[]{:S(2)}) async-start(bf16[64,16,512]{2,1,0:T(8,128)(2,1)} %bitcast.42), calls=%async_computation.4 | async-start | bytes 2097152 | tf_op jit(solution)/shard_map/all_to_all | solution.py:17
  120.6 7.8 %fusion.31 = bf16[1024,512]{1,0:T(8,128)(2,1)} fusion(bf16[1,2048,512]{2,1,0:T(8,128)(2,1)} %param.13, f32[1024,2048]{1,0:T(8,128)} %fusion.16), kind=kOutput, calls=%fused_computation.26 | convolution fusion | flops 2166882304 | bytes 11534336 | tf_op jit(solution)/shard_map/dot_general | solution.py:13
  128.4 20.7 %all-to-all-done.4 = bf16[64,16,512]{2,1,0:T(8,128)(2,1)} async-done(((bf16[64,16,512]{2,1,0:T(8,128)(2,1)}), bf16[64,16,512]{2,1,0:T(8,128)(2,1)}, u32[]{:S(2)}, u32[]{:S(2)}) %all-to-all-start.4) | async-done | bytes 1048608 | tf_op jit(solution)/shard_map/all_to_all | solution.py:17
  149.1 6.4 %all-to-all-start.2 = ((bf16[64,16,512]{2,1,0:T(8,128)(2,1)}), bf16[64,16,512]{2,1,0:T(8,128)(2,1)}, u32[]{:S(2)}, u32[]{:S(2)}) async-start(bf16[64,16,512]{2,1,0:T(8,128)(2,1)} %bitcast.40), calls=%async_computation.2 | async-start | bytes 2097152 | tf_op jit(solution)/shard_map/all_to_all | solution.py:17
  155.5 2.0 fusion.36
  157.5 0.0 copy-start.1
  157.5 0.4 multiply_reduce_fusion
  157.8 0.2 multiply_convert_fusion.4
  158.1 0.4 fusion.51
  158.4 0.0 copy-done.1
  158.4 1.3 fusion.40
  159.8 0.8 reshape.65
  160.6 23.4 %all-to-all-done.2 = bf16[64,16,512]{2,1,0:T(8,128)(2,1)} async-done(((bf16[64,16,512]{2,1,0:T(8,128)(2,1)}), bf16[64,16,512]{2,1,0:T(8,128)(2,1)}, u32[]{:S(2)}, u32[]{:S(2)}) %all-to-all-start.2) | async-done | bytes 1048608 | tf_op jit(solution)/shard_map/all_to_all | solution.py:17
  183.9 6.2 %all-to-all-start.5 = ((bf16[64,4,512]{2,1,0:T(4,128)(2,1)}), bf16[64,4,512]{2,1,0:T(4,128)(2,1)S(1)}, u32[]{:S(2)}, u32[]{:S(2)}) async-start(bf16[64,4,512]{2,1,0:T(4,128)(2,1)} %reshape.65), calls=%async_computation.5 | async-start | bytes 524288 | tf_op jit(solution)/shard_map/all_to_all | solution.py:17
  190.1 2.2 %fusion.38 = bf16[512,512]{1,0:T(8,128)(2,1)} fusion(bf16[512,256]{0,1:T(8,128)(2,1)S(1)} %multiply_convert_fusion.4, bf16[256,512]{1,0:T(8,128)(2,1)S(1)} %reshape.56, bf16[512,512]{1,0:T(8,128)(2,1)} %copy-done.1), kind=kOutput, calls=%fused_computation.33 | convolution fusion | flops 135266304 | bytes 1572864 | tf_op jit(solution)/shard_map/dot_general | solution.py:13
  192.3 2.8 %fusion.35 = bf16[512,512]{1,0:T(8,128)(2,1)} fusion(bf16[1024,512]{1,0:T(8,128)(2,1)} %bitcast.5, s32[512]{0:T(512)S(1)} %get-tuple-element.7), kind=kOutput, calls=%fused_computation.30 | convolution fusion | flops 537657344 | bytes 1574912 | tf_op jit(solution)/shard_map/dot_general | solution.py:13
  195.1 7.1 %all-to-all-done.5 = bf16[64,4,512]{2,1,0:T(4,128)(2,1)S(1)} async-done(((bf16[64,4,512]{2,1,0:T(4,128)(2,1)}), bf16[64,4,512]{2,1,0:T(4,128)(2,1)S(1)}, u32[]{:S(2)}, u32[]{:S(2)}) %all-to-all-start.5) | async-done | bytes 262176 | tf_op jit(solution)/shard_map/all_to_all | solution.py:17
  202.1 0.7 convert_reduce_fusion
  (1 shorter events, 0.0 us)
Async XLA Ops:
  0.6 72.6 %copy-start = (bf16[1,512,2048]{2,1,0:T(8,128)(2,1)S(1)}, bf16[1,512,2048]{2,1,0:T(8,128)(2,1)}, u32[]{:S(2)}) copy-start(bf16[1,512,2048]{2,1,0:T(8,128)(2,1)} %param.12) | copy-start | bytes 6291460
  2.3 25.2 %all-to-all-start = ((bf16[64,4,512]{2,1,0:T(4,128)(2,1)}), bf16[64,4,512]{2,1,0:T(4,128)(2,1)S(1)}, u32[]{:S(2)}, u32[]{:S(2)}) async-start(bf16[64,4,512]{2,1,0:T(4,128)(2,1)} %broadcast_in_dim.6), calls=%async_computation | async-start | bytes 524288 | tf_op jit(solution)/shard_map/all_to_all | solution.py:17
  32.2 34.7 %all-to-all-start.1 = ((bf16[64,16,512]{2,1,0:T(8,128)(2,1)}), bf16[64,16,512]{2,1,0:T(8,128)(2,1)}, u32[]{:S(2)}, u32[]{:S(2)}) async-start(bf16[64,16,512]{2,1,0:T(8,128)(2,1)} %bitcast.43), calls=%async_computation.1 | async-start | bytes 2097152 | tf_op jit(solution)/shard_map/all_to_all | solution.py:17
  66.9 34.9 %all-to-all-start.3 = ((bf16[64,16,512]{2,1,0:T(8,128)(2,1)}), bf16[64,16,512]{2,1,0:T(8,128)(2,1)}, u32[]{:S(2)}, u32[]{:S(2)}) async-start(bf16[64,16,512]{2,1,0:T(8,128)(2,1)} %bitcast.41), calls=%async_computation.3 | async-start | bytes 2097152 | tf_op jit(solution)/shard_map/all_to_all | solution.py:17
  114.2 34.9 %all-to-all-start.4 = ((bf16[64,16,512]{2,1,0:T(8,128)(2,1)}), bf16[64,16,512]{2,1,0:T(8,128)(2,1)}, u32[]{:S(2)}, u32[]{:S(2)}) async-start(bf16[64,16,512]{2,1,0:T(8,128)(2,1)} %bitcast.42), calls=%async_computation.4 | async-start | bytes 2097152 | tf_op jit(solution)/shard_map/all_to_all | solution.py:17
  149.1 34.9 %all-to-all-start.2 = ((bf16[64,16,512]{2,1,0:T(8,128)(2,1)}), bf16[64,16,512]{2,1,0:T(8,128)(2,1)}, u32[]{:S(2)}, u32[]{:S(2)}) async-start(bf16[64,16,512]{2,1,0:T(8,128)(2,1)} %bitcast.40), calls=%async_computation.2 | async-start | bytes 2097152 | tf_op jit(solution)/shard_map/all_to_all | solution.py:17
  157.5 1.0 copy-start.1
  183.9 18.2 %all-to-all-start.5 = ((bf16[64,4,512]{2,1,0:T(4,128)(2,1)}), bf16[64,4,512]{2,1,0:T(4,128)(2,1)S(1)}, u32[]{:S(2)}, u32[]{:S(2)}) async-start(bf16[64,4,512]{2,1,0:T(4,128)(2,1)} %reshape.65), calls=%async_computation.5 | async-start | bytes 524288 | tf_op jit(solution)/shard_map/all_to_all | solution.py:17

commit v2 on v1

v2 whole, which is shorter than its diff:
```python
import functools
import math

import jax
import jax.numpy as jnp
from jax import lax
from jax.experimental import pallas as pl
from jax.experimental.pallas import tpu as pltpu
from jax.sharding import PartitionSpec as P

US = 32
REQ_DEV = 8
LANES = 128
MIB = 1024 * 1024


def dot(a, b, dims=((1,), (0,))):
    return lax.dot_general(a, b, (dims, ((), ())), preferred_element_type=jnp.float32)


def iota(shape, dim):
    return lax.broadcasted_iota(jnp.int32, shape, dim)


def as_column(row):
    size = row.shape[1]
    eye = iota((size, size), 0) == iota((size, size), 1)
    return jnp.sum(jnp.where(eye, row, 0.0), axis=1, keepdims=True)


def read_rows(ref, first, count, width):
    blocks = ref.shape[0]
    chunks = [
        ref[:, first + c * count : first + (c + 1) * count, :].reshape(blocks * count, LANES)
        for c in range(width // LANES)
    ]
    return jnp.concatenate(chunks, axis=1)


def write_rows(ref, first, count, rows):
    blocks = ref.shape[0]
    for c in range(rows.shape[1] // LANES):
        ref[:, first + c * count : first + (c + 1) * count, :] = rows[:, c * LANES : (c + 1) * LANES].reshape(
            blocks, count, LANES
        )


def pack_kernel(capacity, ids_ref, req_ref, emb_ref, grad_ref, user_ref, send_ref, place_ref):
    experts = send_ref.shape[0]
    count, width = emb_ref.shape
    chunks = width // LANES
    ids = ids_ref[...].astype(jnp.float32)
    named = (iota((experts, count), 0).astype(jnp.float32) == ids).astype(jnp.bfloat16)
    earlier = (iota((count, count), 0) < iota((count, count), 1)).astype(jnp.bfloat16)
    slot = jnp.sum(named.astype(jnp.float32) * dot(named, earlier), axis=0, keepdims=True)
    place = ids * capacity + slot
    place_ref[...] = place
    spread = (iota((experts * capacity, count), 0).astype(jnp.float32) == place).astype(jnp.bfloat16)
    write_rows(send_ref, 0, capacity, dot(spread, emb_ref[...]).astype(jnp.bfloat16))
    write_rows(send_ref, chunks * capacity, capacity, dot(spread, grad_ref[...]).astype(jnp.bfloat16))
    first = 2 * chunks * capacity
    at_slot = iota((count, LANES), 1).astype(jnp.float32) == as_column(slot)
    requests = dot(named, jnp.where(at_slot, as_column(req_ref[...].astype(jnp.float32)), 0.0).astype(jnp.bfloat16))
    own = user_ref.shape[0]
    user = jnp.concatenate([user_ref[:, c * LANES : (c + 1) * LANES] for c in range(chunks)], axis=0)
    tail = send_ref.shape[1] - first
    user_tail = jnp.concatenate(
        [user.astype(jnp.float32), jnp.zeros((tail - chunks * own, LANES), jnp.float32)], axis=0
    )
    is_request = iota((experts, tail, LANES), 1) == chunks * own
    send_ref[:, first:, :] = jnp.where(is_request, requests[:, None, :], user_tail[None]).astype(jnp.bfloat16)


def work_kernel(capacity, own, recv_ref, w_in_ref, w_out_ref, send_ref):
    sources = recv_ref.shape[0]
    width, hidden_width = w_in_ref.shape
    chunks = width // LANES
    count = sources * capacity
    scale = 1.0 / math.sqrt(width)
    emb = read_rows(recv_ref, 0, capacity, width)
    grad = read_rows(recv_ref, chunks * capacity, capacity, width)
    first = 2 * chunks * capacity
    keys_n = sources * own
    user_rows = chunks * own
    flat = recv_ref[:, first : first + user_rows, :].reshape(sources * user_rows, LANES)
    key_of = iota((keys_n, sources * user_rows), 0)
    row_of = iota((keys_n, sources * user_rows), 1)
    keys = jnp.concatenate(
        [
            dot((row_of == key_of // own * user_rows + c * own + key_of % own).astype(jnp.bfloat16), flat)
            for c in range(chunks)
        ],
        axis=1,
    ).astype(jnp.bfloat16)
    requests = recv_ref[:, first + user_rows, :].astype(jnp.bfloat16)
    source_of = (iota((count, sources), 0) // capacity == iota((count, sources), 1)).astype(jnp.bfloat16)
    spread = dot(source_of, requests)
    mine = iota((count, LANES), 1) == iota((count, LANES), 0) % capacity
    request = jnp.sum(jnp.where(mine, spread, 0.0), axis=1, keepdims=True)
    member = (iota((count, keys_n), 1) // US).astype(jnp.float32) == request

    scores = dot(emb, keys, ((1,), (1,))) * scale
    peak = jnp.max(jnp.where(member, scores, -jnp.inf), axis=1, keepdims=True)
    weights = jnp.exp(jnp.where(member, scores - peak, -jnp.inf))
    probs = weights / jnp.sum(weights, axis=1, keepdims=True)
    probs_b = probs.astype(jnp.bfloat16)
    inputs = (emb.astype(jnp.float32) + dot(probs_b, keys)).astype(jnp.bfloat16)

    c0 = math.sqrt(2.0 / math.pi)
    out = jnp.zeros((count, width), jnp.float32)
    back_in = jnp.zeros((count, width), jnp.float32)
    step = 256
    for f in range(0, hidden_width, step):
        first_w = w_in_ref[:, f : f + step]
        second_w = w_out_ref[f : f + step, :]
        pre = dot(inputs, first_w)
        back = dot(grad, second_w, ((1,), (1,)))
        square = pre * pre
        half = 0.5 + 0.5 * jnp.tanh(pre * (c0 + (c0 * 0.044715) * square))
        gelu = pre * half
        slope_g = half + gelu * (1.0 - half) * (2.0 * c0 + (6.0 * c0 * 0.044715) * square)
        out = out + dot(gelu.astype(jnp.bfloat16), second_w)
        back_in = back_in + dot((back * slope_g).astype(jnp.bfloat16), first_w, ((1,), (1,)))
    write_rows(send_ref, 0, capacity, out.astype(jnp.bfloat16))
    d_in = back_in.astype(jnp.bfloat16)

    d_probs = dot(d_in, keys, ((1,), (1,)))
    center = jnp.sum(probs * d_probs, axis=1, keepdims=True)
    slope = (probs * (d_probs - center)).astype(jnp.bfloat16)
    cand_grad = d_in.astype(jnp.float32) + dot(slope, keys) * scale
    write_rows(send_ref, chunks * capacity, capacity, cand_grad.astype(jnp.bfloat16))
    share = dot(probs_b, d_in, ((0,), (0,))) + dot(slope, emb, ((0,), (0,))) * scale
    share = share.astype(jnp.bfloat16)
    place_of = iota((sources * user_rows, keys_n), 0)
    from_key = iota((sources * user_rows, keys_n), 1)
    tail = jnp.zeros((sources * user_rows, LANES), jnp.float32)
    for c in range(chunks):
        pick = place_of == from_key // own * user_rows + c * own + from_key % own
        tail = tail + dot(pick.astype(jnp.bfloat16), share[:, c * LANES : (c + 1) * LANES])
    send_ref[:, first : first + user_rows, :] = tail.reshape(sources, user_rows, LANES).astype(jnp.bfloat16)


def unpack_kernel(capacity, own, recv_ref, place_ref, out_ref, grad_ref, user_ref):
    experts = recv_ref.shape[0]
    count, width = out_ref.shape
    chunks = width // LANES
    place = as_column(place_ref[...])
    pick = (iota((count, experts * capacity), 1).astype(jnp.float32) == place).astype(jnp.bfloat16)
    out_ref[...] = dot(pick, read_rows(recv_ref, 0, capacity, width)).astype(jnp.bfloat16)
    grad_ref[...] = dot(pick, read_rows(recv_ref, chunks * capacity, capacity, width)).astype(jnp.bfloat16)
    first = 2 * chunks * capacity
    total = jnp.sum(recv_ref[:, first:, :].astype(jnp.float32), axis=0)
    for c in range(chunks):
        user_ref[:, c * LANES : (c + 1) * LANES] = total[c * own : (c + 1) * own, :]


def exchange(blocks):
    return lax.all_to_all(blocks, "cand", split_axis=0, concat_axis=0, tiled=True)


def shards(cand_emb, cand_req, expert_ids, user_state, d_out, w_in, w_out):
    count, width = cand_emb.shape
    own = user_state.shape[0]
    experts = lax.axis_size("cand") * w_in.shape[0]
    capacity = 2 * count // experts
    chunks = width // LANES
    body = chunks * (2 * capacity + own)
    there = body + 8
    local_req = cand_req - lax.axis_index("req") * REQ_DEV
    send, place = pl.pallas_call(
        functools.partial(pack_kernel, capacity),
        out_shape=(
            jax.ShapeDtypeStruct((experts, there, LANES), jnp.bfloat16),
            jax.ShapeDtypeStruct((1, count), jnp.float32),
        ),
        compiler_params=pltpu.CompilerParams(vmem_limit_bytes=24 * MIB),
        name="pack",
    )(expert_ids[None], local_req[None], cand_emb, d_out, user_state)
    recv = exchange(send)
    send = pl.pallas_call(
        functools.partial(work_kernel, capacity, own),
        out_shape=jax.ShapeDtypeStruct((experts, body, LANES), jnp.bfloat16),
        scratch_shapes=[],
        compiler_params=pltpu.CompilerParams(vmem_limit_bytes=56 * MIB),
        name="work",
    )(recv, w_in[0], w_out[0])
    recv = exchange(send)
    tower_out, cand_grad, user_grad = pl.pallas_call(
        functools.partial(unpack_kernel, capacity, own),
        out_shape=(
            jax.ShapeDtypeStruct((count, width), jnp.bfloat16),
            jax.ShapeDtypeStruct((count, width), jnp.bfloat16),
            jax.ShapeDtypeStruct((own, width), jnp.float32),
        ),
        compiler_params=pltpu.CompilerParams(vmem_limit_bytes=24 * MIB),
        name="unpack",
    )(recv, place)
    return (tower_out, cand_grad, user_grad)


def solution(mesh):
    rows = P(("req", "cand"), None)
    ids = P(("req", "cand"))
    weights = P("cand", None, None)
    in_specs = (rows, ids, ids, rows, rows, weights, weights)
    return jax.shard_map(shards, mesh=mesh, in_specs=in_specs, out_specs=(rows, rows, rows), check_vma=False)
```

time: 204 us -> 163 us (0.80)
  blocking collectives: 0 us -> 136 us
  waiting for transfers between devices: 109 us -> 0 us
  starting transfers between devices: 44.7 us -> 0 us
  matrix products: 44.3 us -> 0 us
  Pallas kernels: 0 us -> 22 us
    all_to_all x0 -> x2, blocking collectives: none -> 136 us  [exchange(): lax.all_to_all(blocks, 'cand', split_axis=0, concat_axis=0, tiled=True)]
    all_to_all x6 -> x0, waiting for transfers between devices: 109 us -> none  [exchange(): lax.all_to_all(blocks, 'cand', split_axis=0, concat_axis=0, tiled=True)]
    all_to_all x6 -> x0, starting transfers between devices: 44.7 us -> none  [exchange(): lax.all_to_all(blocks, 'cand', split_axis=0, concat_axis=0, tiled=True)]
    dot_general x13 -> x0, matrix products: 44.3 us -> none  [dot(): lax.dot_general(a, b, (dims, ((), ())), preferred_element_type=jnp.float32)]
    pallas_call x0 -> x3, Pallas kernels: none -> 22 us  [the longest x1 18.3 us: shards(): pl.pallas_call(functools.partial(work_kernel, capacity, own), out_shape=j...]
    unnamed x4 -> x8, local copies, waits for them, and re-layouts: 0.02 us -> 3.45 us
  transfers between devices with their start and end apart: 6 -> 0, of which waited for: 6 -> 0; matrix products, arithmetic and copies ran while one was open for 14% -> 0% of each run, Pallas kernels for 0% -> 0%
where the time goes in v2:
time: 163 us
  blocking collectives  136 us (83%)
  Pallas kernels  22 us (13%)
  local copies, waits for them, and re-layouts  3.45 us (2%)
    all_to_all x2, blocking collectives, exchange(): lax.all_to_all(blocks, 'cand', split_axis=0, concat_axis=0, tiled=True)  136 us
    pallas_call x1, Pallas kernels, shards(): pl.pallas_call(functools.partial(work_kernel, capacity, own), out_shape=j...  18.3 us
    unnamed x8, local copies, waits for them, and re-layouts  3.45 us

profile of v2, /device:TPU:1, one launch (start us, length us, event | category | flops | bytes accessed | tf_op | source)
XLA Modules:
  0.0 162.5 jit_solution(8984014167392115109)
XLA Ops:
  0.6 0.7 broadcast_subtract_fusion
  1.3 0.0 copy-start
  1.3 1.0 copy-done
  2.4 0.0 copy-start.1
  2.4 1.0 copy-done.1
  3.4 0.0 copy-start.2
  3.4 0.7 copy-done.2
  4.1 0.0 copy-start.3
  4.1 0.7 copy-done.3
  4.8 1.5 pack.1
  6.3 72.7 %all_to_all.10.recv_ref = bf16[64,152,128]{2,1,0:T(8,128)(2,1)} all-to-all(bf16[64,152,128]{2,1,0:T(8,128)(2,1)S(1)} %get-tuple-element.5), channel_id=1, replica_groups=mesh['req'=4,'cand'=64] {'cand'}, dimensions={0} | all-to-all | bytes 4980736 | tf_op jit(solution)/shard_map/all_to_all | solution.py:158
  79.0 18.3 %work.1 = bf16[64,144,128]{2,1,0:T(8,128)(2,1)} custom-call(bf16[64,152,128]{2,1,0:T(8,128)(2,1)} %all_to_all.10.recv_ref, bf16[512,2048]{1,0:T(8,128)(2,1)} %bitcast.6, bf16[2048,512]{1,0:T(8,128)(2,1)} %bitcast.7), custom_call_target="tpu_custom_call" | custom-call | tf_op jit(solution)/shard_map/work/pallas_call | solution.py:180
  97.3 63.1 %all_to_all.11.recv_ref = bf16[64,144,128]{2,1,0:T(8,128)(2,1)S(1)} all-to-all(bf16[64,144,128]{2,1,0:T(8,128)(2,1)} %work.1), channel_id=1, replica_groups=mesh['req'=4,'cand'=64] {'cand'}, dimensions={0} | all-to-all | bytes 4718592 | tf_op jit(solution)/shard_map/all_to_all | solution.py:158
  160.4 2.1 %unpack.1 = (bf16[512,512]{1,0:T(8,128)(2,1)}, bf16[512,512]{1,0:T(8,128)(2,1)}, f32[4,512]{1,0:T(4,128)}) custom-call(bf16[64,144,128]{2,1,0:T(8,128)(2,1)S(1)} %all_to_all.11.recv_ref, f32[1,512]{1,0:T(1,128)S(1)} %get-tuple-element.6.place_ref), custom_call_target="tpu_custom_call" | custom-call | tf_op jit(solution)/shard_map/unpack/pallas_call | solution.py:188
Async XLA Ops:
  1.3 1.0 copy-start
  2.4 1.0 copy-start.1
  3.4 0.7 copy-start.2
  4.1 0.7 copy-start.3

commit v3 on v2

v3 whole, which is shorter than its diff:
```python
import functools
import math

import jax
import jax.numpy as jnp
from jax import lax
from jax.experimental import pallas as pl
from jax.experimental.pallas import tpu as pltpu
from jax.sharding import PartitionSpec as P

US = 32
REQ_DEV = 8
LANES = 128
MIB = 1024 * 1024


def dot(a, b, dims=((1,), (0,))):
    return lax.dot_general(a, b, (dims, ((), ())), preferred_element_type=jnp.float32)


def iota(shape, dim):
    return lax.broadcasted_iota(jnp.int32, shape, dim)


def as_column(row):
    size = row.shape[1]
    eye = iota((size, size), 0) == iota((size, size), 1)
    return jnp.sum(jnp.where(eye, row, 0.0), axis=1, keepdims=True)


def read_rows(ref, first, count, width):
    blocks = ref.shape[0]
    chunks = [
        ref[:, first + c * count : first + (c + 1) * count, :].reshape(blocks * count, LANES)
        for c in range(width // LANES)
    ]
    return jnp.concatenate(chunks, axis=1)


def write_rows(ref, first, count, rows):
    blocks = ref.shape[0]
    for c in range(rows.shape[1] // LANES):
        ref[:, first + c * count : first + (c + 1) * count, :] = rows[:, c * LANES : (c + 1) * LANES].reshape(
            blocks, count, LANES
        )


def pack_kernel(
    capacity, ids_hbm, req_hbm, emb_hbm, grad_hbm, user_hbm, send_hbm, place_ref,
    ids_ref, req_ref, emb_ref, grad_ref, user_ref, send_ref, sems, out_sems,
):
    pairs = (
        (ids_hbm, ids_ref), (req_hbm, req_ref), (user_hbm, user_ref), (emb_hbm, emb_ref), (grad_hbm, grad_ref),
    )
    copies = [pltpu.make_async_copy(src, dst, sems.at[i]) for i, (src, dst) in enumerate(pairs)]
    for copy in copies:
        copy.start()
    experts = send_ref.shape[0]
    count, width = emb_ref.shape
    chunks = width // LANES
    own = user_ref.shape[0]
    earlier = (iota((count, count), 0) < iota((count, count), 1)).astype(jnp.bfloat16)
    copies[0].wait()
    ids = ids_ref[...].astype(jnp.float32)
    named = (iota((experts, count), 0).astype(jnp.float32) == ids).astype(jnp.bfloat16)
    slot = jnp.sum(named.astype(jnp.float32) * dot(named, earlier), axis=0, keepdims=True)
    place = ids * capacity + slot
    place_ref[...] = place
    copies[1].wait()
    copies[2].wait()
    first = 2 * chunks * capacity
    local_req = (req_ref[...] & (REQ_DEV - 1)).astype(jnp.float32)
    at_slot = iota((count, LANES), 1).astype(jnp.float32) == as_column(slot)
    requests = dot(named, jnp.where(at_slot, as_column(local_req), 0.0).astype(jnp.bfloat16))
    user = jnp.concatenate([user_ref[:, c * LANES : (c + 1) * LANES] for c in range(chunks)], axis=0)
    tail = send_ref.shape[1] - first
    user_tail = jnp.concatenate(
        [user.astype(jnp.float32), jnp.zeros((tail - chunks * own, LANES), jnp.float32)], axis=0
    )
    is_request = iota((experts, tail, LANES), 1) == chunks * own
    send_ref[:, first:, :] = jnp.where(is_request, requests[:, None, :], user_tail[None]).astype(jnp.bfloat16)
    copies[3].wait()
    copies[4].wait()
    parts = out_sems.shape[0]
    blocks = experts // parts
    slot_of = iota((blocks * capacity, count), 0).astype(jnp.float32)
    outs = []
    for p in range(parts):
        spread = (slot_of == place - float(p * blocks * capacity)).astype(jnp.bfloat16)
        part = send_ref.at[p * blocks : (p + 1) * blocks]
        write_rows(part, 0, capacity, dot(spread, emb_ref[...]).astype(jnp.bfloat16))
        write_rows(part, chunks * capacity, capacity, dot(spread, grad_ref[...]).astype(jnp.bfloat16))
        outs.append(pltpu.make_async_copy(part, send_hbm.at[p * blocks : (p + 1) * blocks], out_sems.at[p]))
        outs[p].start()
    for copy in outs:
        copy.wait()


def work_kernel(capacity, own, recv_ref, w_in_ref, w_out_ref, send_ref):
    sources = recv_ref.shape[0]
    width = w_in_ref.shape[0]
    chunks = width // LANES
    count = sources * capacity
    scale = 1.0 / math.sqrt(width)
    emb = read_rows(recv_ref, 0, capacity, width)
    grad = read_rows(recv_ref, chunks * capacity, capacity, width)
    first = 2 * chunks * capacity
    keys_n = sources * own
    user_rows = chunks * own
    users = recv_ref[:, first : first + user_rows, :].astype(jnp.float32)
    keys = jnp.concatenate(
        [users[:, c * own : (c + 1) * own, :].reshape(keys_n, LANES) for c in range(chunks)], axis=1
    ).astype(jnp.bfloat16)
    requests = recv_ref[:, first + user_rows, :].astype(jnp.bfloat16)
    source_of = (iota((count, sources), 0) // capacity == iota((count, sources), 1)).astype(jnp.bfloat16)
    spread = dot(source_of, requests)
    mine = iota((count, LANES), 1) == iota((count, LANES), 0) % capacity
    request = jnp.sum(jnp.where(mine, spread, 0.0), axis=1, keepdims=True)
    member = (iota((count, keys_n), 1) // US).astype(jnp.float32) == request

    scores = dot(emb, keys, ((1,), (1,))) * scale
    peak = jnp.max(jnp.where(member, scores, -jnp.inf), axis=1, keepdims=True)
    weights = jnp.exp(jnp.where(member, scores - peak, -jnp.inf))
    probs = weights / jnp.sum(weights, axis=1, keepdims=True)
    probs_b = probs.astype(jnp.bfloat16)
    inputs = (emb.astype(jnp.float32) + dot(probs_b, keys)).astype(jnp.bfloat16)

    c0 = math.sqrt(2.0 / math.pi)
    outs, backs = [], []
    tile = count // 4
    for m in range(0, count, tile):
        pre = dot(inputs[m : m + tile], w_in_ref[...])
        back = dot(grad[m : m + tile], w_out_ref[...], ((1,), (1,)))
        square = pre * pre
        half = 0.5 + 0.5 * jnp.tanh(pre * (c0 + (c0 * 0.044715) * square))
        gelu = pre * half
        slope_g = half + gelu * (1.0 - half) * (2.0 * c0 + (6.0 * c0 * 0.044715) * square)
        outs.append(dot(gelu.astype(jnp.bfloat16), w_out_ref[...]).astype(jnp.bfloat16))
        backs.append(dot((back * slope_g).astype(jnp.bfloat16), w_in_ref[...], ((1,), (1,))).astype(jnp.bfloat16))
    write_rows(send_ref, 0, capacity, jnp.concatenate(outs, axis=0))
    d_in = jnp.concatenate(backs, axis=0)

    d_probs = dot(d_in, keys, ((1,), (1,)))
    center = jnp.sum(probs * d_probs, axis=1, keepdims=True)
    slope = (probs * (d_probs - center)).astype(jnp.bfloat16)
    cand_grad = d_in.astype(jnp.float32) + dot(slope, keys) * scale
    write_rows(send_ref, chunks * capacity, capacity, cand_grad.astype(jnp.bfloat16))
    share = dot(probs_b, d_in, ((0,), (0,))) + dot(slope, emb, ((0,), (0,))) * scale
    tail = jnp.concatenate(
        [share[:, c * LANES : (c + 1) * LANES].reshape(sources, own, LANES) for c in range(chunks)], axis=1
    )
    send_ref[:, first : first + user_rows, :] = tail.astype(jnp.bfloat16)


def unpack_kernel(capacity, own, recv_ref, place_ref, out_hbm, grad_hbm, user_hbm, out_ref, grad_ref, user_ref, sems):
    experts = recv_ref.shape[0]
    count, width = out_ref.shape
    chunks = width // LANES
    first = 2 * chunks * capacity
    total = jnp.sum(recv_ref[:, first:, :].astype(jnp.float32), axis=0)
    for c in range(chunks):
        user_ref[:, c * LANES : (c + 1) * LANES] = total[c * own : (c + 1) * own, :]
    copies = [pltpu.make_async_copy(user_ref, user_hbm, sems.at[0])]
    copies[0].start()
    place = as_column(place_ref[...])
    pick = (iota((count, experts * capacity), 1).astype(jnp.float32) == place).astype(jnp.bfloat16)
    out_ref[...] = dot(pick, read_rows(recv_ref, 0, capacity, width)).astype(jnp.bfloat16)
    copies.append(pltpu.make_async_copy(out_ref, out_hbm, sems.at[1]))
    copies[1].start()
    grads = read_rows(recv_ref, chunks * capacity, capacity, width)
    part = count // 2
    for p in range(2):
        rows = pl.ds(p * part, part)
        grad_ref[rows, :] = dot(pick[p * part : (p + 1) * part], grads).astype(jnp.bfloat16)
        copies.append(pltpu.make_async_copy(grad_ref.at[rows, :], grad_hbm.at[rows, :], sems.at[2 + p]))
        copies[2 + p].start()
    for copy in copies:
        copy.wait()


def exchange(blocks):
    return lax.all_to_all(blocks, "cand", split_axis=0, concat_axis=0, tiled=True)


def shards(cand_emb, cand_req, expert_ids, user_state, d_out, w_in, w_out):
    count, width = cand_emb.shape
    own = user_state.shape[0]
    experts = lax.axis_size("cand") * w_in.shape[0]
    capacity = 2 * count // experts
    chunks = width // LANES
    body = chunks * (2 * capacity + own)
    there = body + 8
    hbm = pl.BlockSpec(memory_space=pltpu.HBM)
    send, place = pl.pallas_call(
        functools.partial(pack_kernel, capacity),
        in_specs=[hbm] * 5,
        out_shape=(
            jax.ShapeDtypeStruct((experts, there, LANES), jnp.bfloat16),
            jax.ShapeDtypeStruct((1, count), jnp.float32),
        ),
        out_specs=(hbm, pl.BlockSpec(memory_space=pltpu.VMEM)),
        scratch_shapes=[
            pltpu.VMEM((1, count), jnp.int32),
            pltpu.VMEM((1, count), jnp.int32),
            pltpu.VMEM((count, width), jnp.bfloat16),
            pltpu.VMEM((count, width), jnp.bfloat16),
            pltpu.VMEM((own, width), jnp.bfloat16),
            pltpu.VMEM((experts, there, LANES), jnp.bfloat16),
            pltpu.SemaphoreType.DMA((5,)),
            pltpu.SemaphoreType.DMA((4,)),
        ],
        compiler_params=pltpu.CompilerParams(vmem_limit_bytes=60 * MIB),
        name="pack",
    )(expert_ids[None], cand_req[None], cand_emb, d_out, user_state)
    recv = exchange(send)
    send = pl.pallas_call(
        functools.partial(work_kernel, capacity, own),
        out_shape=jax.ShapeDtypeStruct((experts, body, LANES), jnp.bfloat16),
        compiler_params=pltpu.CompilerParams(vmem_limit_bytes=30 * MIB),
        name="work",
    )(recv, w_in[0], w_out[0])
    recv = exchange(send)
    outs = (
        jax.ShapeDtypeStruct((count, width), jnp.bfloat16),
        jax.ShapeDtypeStruct((count, width), jnp.bfloat16),
        jax.ShapeDtypeStruct((own, width), jnp.float32),
    )
    tower_out, cand_grad, user_grad = pl.pallas_call(
        functools.partial(unpack_kernel, capacity, own),
        out_shape=outs,
        out_specs=(hbm, hbm, hbm),
        scratch_shapes=[pltpu.VMEM(o.shape, o.dtype) for o in outs] + [pltpu.SemaphoreType.DMA((4,))],
        compiler_params=pltpu.CompilerParams(vmem_limit_bytes=24 * MIB),
        name="unpack",
    )(recv, place)
    return (tower_out, cand_grad, user_grad)


def solution(mesh):
    rows = P(("req", "cand"), None)
    ids = P(("req", "cand"))
    weights = P("cand", None, None)
    in_specs = (rows, ids, ids, rows, rows, weights, weights)
    return jax.shard_map(shards, mesh=mesh, in_specs=in_specs, out_specs=(rows, rows, rows), check_vma=False)
```

time: 163 us -> 155 us (0.951)
  Pallas kernels: 22 us -> 18.3 us
  local copies, waits for them, and re-layouts: 3.45 us -> 0.02 us
    pallas_call x1, Pallas kernels: 18.3 us -> 12 us  [shards(): pl.pallas_call(functools.partial(work_kernel, capacity, own), out_shape=j...]
    unnamed x8 -> x6, local copies, waits for them, and re-layouts: 3.45 us -> 0.02 us
    pallas_call x1, Pallas kernels: 1.53 us -> 4.05 us  [shards(): pl.pallas_call(functools.partial(pack_kernel, capacity), in_specs=[hbm] *...]
where the time goes in v3:
time: 155 us
  blocking collectives  136 us (88%)
  Pallas kernels  18.3 us (12%)
    all_to_all x2, blocking collectives, exchange(): lax.all_to_all(blocks, 'cand', split_axis=0, concat_axis=0, tiled=True)  136 us
    pallas_call x1, Pallas kernels, shards(): pl.pallas_call(functools.partial(work_kernel, capacity, own), out_shape=j...  12 us
    pallas_call x1, Pallas kernels, shards(): pl.pallas_call(functools.partial(pack_kernel, capacity), in_specs=[hbm] *...  4.05 us

profile of v3, /device:TPU:1, one launch (start us, length us, event | category | flops | bytes accessed | tf_op | source)
XLA Modules:
  0.0 155.1 jit_solution(4611100211021848976)
XLA Ops:
  0.6 4.0 %pack.1 = (bf16[64,152,128]{2,1,0:T(8,128)(2,1)}, f32[1,512]{1,0:T(1,128)}) custom-call(s32[1,512]{1,0:T(1,128)} %bitcast.6, s32[1,512]{1,0:T(1,128)} %bitcast.7, bf16[512,512]{1,0:T(8,128)(2,1)} %emb_hbm.1, bf16[512,512]{1,0:T(8,128)(2,1)} %grad_hbm.1, bf16[4,512]{1,0:T(4,128)(2,1)} %user_hbm.1), custom_call_target="tpu_custom_call" | custom-call | tf_op jit(solution)/shard_map/pack/pallas_call | solution.py:194
  4.7 0.0 copy-start
  4.7 0.0 copy-start.1
  4.7 73.0 %all_to_all.10.recv_ref = bf16[64,152,128]{2,1,0:T(8,128)(2,1)S(1)} all-to-all(bf16[64,152,128]{2,1,0:T(8,128)(2,1)} %get-tuple-element.5), channel_id=1, replica_groups=mesh['req'=4,'cand'=64] {'cand'}, dimensions={0} | all-to-all | bytes 4980736 | tf_op jit(solution)/shard_map/all_to_all | solution.py:182
  77.8 0.0 copy-done
  77.8 0.0 copy-done.1
  77.8 12.0 %work.1 = bf16[64,144,128]{2,1,0:T(8,128)(2,1)S(1)} custom-call(bf16[64,152,128]{2,1,0:T(8,128)(2,1)S(1)} %all_to_all.10.recv_ref, bf16[512,2048]{1,0:T(8,128)(2,1)S(1)} %bitcast.4, bf16[2048,512]{1,0:T(8,128)(2,1)S(1)} %bitcast.5), custom_call_target="tpu_custom_call" | custom-call | tf_op jit(solution)/shard_map/work/pallas_call | solution.py:216
  89.8 0.0 copy-start.2
  89.8 62.9 %all_to_all.11.recv_ref = bf16[64,144,128]{2,1,0:T(8,128)(2,1)S(1)} all-to-all(bf16[64,144,128]{2,1,0:T(8,128)(2,1)S(1)} %work.1), channel_id=1, replica_groups=mesh['req'=4,'cand'=64] {'cand'}, dimensions={0} | all-to-all | bytes 4718592 | tf_op jit(solution)/shard_map/all_to_all | solution.py:182
  152.7 0.0 copy-done.2
  152.7 2.3 %unpack.1 = (bf16[512,512]{1,0:T(8,128)(2,1)}, bf16[512,512]{1,0:T(8,128)(2,1)}, f32[4,512]{1,0:T(4,128)}) custom-call(bf16[64,144,128]{2,1,0:T(8,128)(2,1)S(1)} %all_to_all.11.recv_ref, f32[1,512]{1,0:T(1,128)S(1)} %copy-done.2), custom_call_target="tpu_custom_call" | custom-call | tf_op jit(solution)/shard_map/unpack/pallas_call | solution.py:228
Async XLA Ops:
  4.7 73.1 %copy-start = (bf16[1,512,2048]{2,1,0:T(8,128)(2,1)S(1)}, bf16[1,512,2048]{2,1,0:T(8,128)(2,1)}, u32[]{:S(2)}) copy-start(bf16[1,512,2048]{2,1,0:T(8,128)(2,1)} %param.12) | copy-start | bytes 6291460
  4.7 73.1 %copy-start.1 = (bf16[1,2048,512]{2,1,0:T(8,128)(2,1)S(1)}, bf16[1,2048,512]{2,1,0:T(8,128)(2,1)}, u32[]{:S(2)}) copy-start(bf16[1,2048,512]{2,1,0:T(8,128)(2,1)} %param.13) | copy-start | bytes 6291460
  89.8 62.9 %copy-start.2 = (f32[1,512]{1,0:T(1,128)S(1)}, f32[1,512]{1,0:T(1,128)}, u32[]{:S(2)}) copy-start(f32[1,512]{1,0:T(1,128)} %get-tuple-element.6.place_ref) | copy-start | bytes 6148

commit v4 on v3

--- a/solution.py
+++ b/solution.py
@@ -46,8 +46,8 @@
 
 
 def pack_kernel(
-    capacity, ids_hbm, req_hbm, emb_hbm, grad_hbm, user_hbm, send_hbm, place_ref,
-    ids_ref, req_ref, emb_ref, grad_ref, user_ref, send_ref, sems, out_sems,
+    capacity, ids_hbm, req_hbm, emb_hbm, grad_hbm, user_hbm, send_ref, place_ref,
+    ids_ref, req_ref, emb_ref, grad_ref, user_ref, sems,
 ):
     pairs = (
         (ids_hbm, ids_ref), (req_hbm, req_ref), (user_hbm, user_ref), (emb_hbm, emb_ref), (grad_hbm, grad_ref),
@@ -65,7 +65,7 @@
     named = (iota((experts, count), 0).astype(jnp.float32) == ids).astype(jnp.bfloat16)
     slot = jnp.sum(named.astype(jnp.float32) * dot(named, earlier), axis=0, keepdims=True)
     place = ids * capacity + slot
-    place_ref[...] = place
+    place_ref[...] = as_column(place)
     copies[1].wait()
     copies[2].wait()
     first = 2 * chunks * capacity
@@ -81,19 +81,9 @@
     send_ref[:, first:, :] = jnp.where(is_request, requests[:, None, :], user_tail[None]).astype(jnp.bfloat16)
     copies[3].wait()
     copies[4].wait()
-    parts = out_sems.shape[0]
-    blocks = experts // parts
-    slot_of = iota((blocks * capacity, count), 0).astype(jnp.float32)
-    outs = []
-    for p in range(parts):
-        spread = (slot_of == place - float(p * blocks * capacity)).astype(jnp.bfloat16)
-        part = send_ref.at[p * blocks : (p + 1) * blocks]
-        write_rows(part, 0, capacity, dot(spread, emb_ref[...]).astype(jnp.bfloat16))
-        write_rows(part, chunks * capacity, capacity, dot(spread, grad_ref[...]).astype(jnp.bfloat16))
-        outs.append(pltpu.make_async_copy(part, send_hbm.at[p * blocks : (p + 1) * blocks], out_sems.at[p]))
-        outs[p].start()
-    for copy in outs:
-        copy.wait()
+    spread = (iota((experts * capacity, count), 0).astype(jnp.float32) == place).astype(jnp.bfloat16)
+    write_rows(send_ref, 0, capacity, dot(spread, emb_ref[...]).astype(jnp.bfloat16))
+    write_rows(send_ref, chunks * capacity, capacity, dot(spread, grad_ref[...]).astype(jnp.bfloat16))
 
 
 def work_kernel(capacity, own, recv_ref, w_in_ref, w_out_ref, send_ref):
@@ -162,8 +152,7 @@
         user_ref[:, c * LANES : (c + 1) * LANES] = total[c * own : (c + 1) * own, :]
     copies = [pltpu.make_async_copy(user_ref, user_hbm, sems.at[0])]
     copies[0].start()
-    place = as_column(place_ref[...])
-    pick = (iota((count, experts * capacity), 1).astype(jnp.float32) == place).astype(jnp.bfloat16)
+    pick = (iota((count, experts * capacity), 1).astype(jnp.float32) == place_ref[...]).astype(jnp.bfloat16)
     out_ref[...] = dot(pick, read_rows(recv_ref, 0, capacity, width)).astype(jnp.bfloat16)
     copies.append(pltpu.make_async_copy(out_ref, out_hbm, sems.at[1]))
     copies[1].start()
@@ -195,21 +184,18 @@
         functools.partial(pack_kernel, capacity),
         in_specs=[hbm] * 5,
         out_shape=(
-            jax.ShapeDtypeStruct((experts, there, LANES), jnp.bfloat16),
-            jax.ShapeDtypeStruct((1, count), jnp.float32),
+            pltpu.VMEM((experts, there, LANES), jnp.bfloat16),
+            pltpu.VMEM((count, 1), jnp.float32),
         ),
-        out_specs=(hbm, pl.BlockSpec(memory_space=pltpu.VMEM)),
         scratch_shapes=[
             pltpu.VMEM((1, count), jnp.int32),
             pltpu.VMEM((1, count), jnp.int32),
             pltpu.VMEM((count, width), jnp.bfloat16),
             pltpu.VMEM((count, width), jnp.bfloat16),
             pltpu.VMEM((own, width), jnp.bfloat16),
-            pltpu.VMEM((experts, there, LANES), jnp.bfloat16),
             pltpu.SemaphoreType.DMA((5,)),
-            pltpu.SemaphoreType.DMA((4,)),
         ],
-        compiler_params=pltpu.CompilerParams(vmem_limit_bytes=60 * MIB),
+        compiler_params=pltpu.CompilerParams(vmem_limit_bytes=56 * MIB),
         name="pack",
     )(expert_ids[None], cand_req[None], cand_emb, d_out, user_state)
     recv = exchange(send)

time: 155 us -> 154 us (level)
  no operation moved by 1% of the time
where the time goes in v4:
time: 154 us
  blocking collectives  136 us (88%)
  Pallas kernels  17 us (11%)
    all_to_all x2, blocking collectives, exchange(): lax.all_to_all(blocks, 'cand', split_axis=0, concat_axis=0, tiled=True)  136 us
    pallas_call x1, Pallas kernels, shards(): pl.pallas_call(functools.partial(work_kernel, capacity, own), out_shape=j...  12 us

profile of v4, /device:TPU:1, one launch (start us, length us, event | category | flops | bytes accessed | tf_op | source)
XLA Modules:
  0.0 153.5 jit_solution(6483839903194710163)
XLA Ops:
  0.6 2.7 %pack.1 = (bf16[64,152,128]{2,1,0:T(8,128)(2,1)S(1)}, f32[512,1]{1,0:T(8,128)S(1)}) custom-call(s32[1,512]{1,0:T(1,128)} %bitcast.6, s32[1,512]{1,0:T(1,128)} %bitcast.7, bf16[512,512]{1,0:T(8,128)(2,1)} %emb_hbm.1, bf16[512,512]{1,0:T(8,128)(2,1)} %grad_hbm.1, bf16[4,512]{1,0:T(4,128)(2,1)} %user_hbm.1), custom_call_target="tpu_custom_call" | custom-call | tf_op jit(solution)/shard_map/pack/pallas_call | solution.py:183
  3.4 0.0 copy-start
  3.4 0.0 copy-start.1
  3.4 72.8 %all_to_all.10.recv_ref = bf16[64,152,128]{2,1,0:T(8,128)(2,1)S(1)} all-to-all(bf16[64,152,128]{2,1,0:T(8,128)(2,1)S(1)} %get-tuple-element.5), channel_id=1, replica_groups=mesh['req'=4,'cand'=64] {'cand'}, dimensions={0} | all-to-all | bytes 4980736 | tf_op jit(solution)/shard_map/all_to_all | solution.py:171
  76.2 0.0 copy-done
  76.2 0.0 copy-done.1
  76.2 12.0 %work.1 = bf16[64,144,128]{2,1,0:T(8,128)(2,1)S(1)} custom-call(bf16[64,152,128]{2,1,0:T(8,128)(2,1)S(1)} %all_to_all.10.recv_ref, bf16[512,2048]{1,0:T(8,128)(2,1)S(1)} %bitcast.4, bf16[2048,512]{1,0:T(8,128)(2,1)S(1)} %bitcast.5), custom_call_target="tpu_custom_call" | custom-call | tf_op jit(solution)/shard_map/work/pallas_call | solution.py:202
  88.3 62.9 %all_to_all.11.recv_ref = bf16[64,144,128]{2,1,0:T(8,128)(2,1)S(1)} all-to-all(bf16[64,144,128]{2,1,0:T(8,128)(2,1)S(1)} %work.1), channel_id=1, replica_groups=mesh['req'=4,'cand'=64] {'cand'}, dimensions={0} | all-to-all | bytes 4718592 | tf_op jit(solution)/shard_map/all_to_all | solution.py:171
  151.1 2.2 %unpack.1 = (bf16[512,512]{1,0:T(8,128)(2,1)}, bf16[512,512]{1,0:T(8,128)(2,1)}, f32[4,512]{1,0:T(4,128)}) custom-call(bf16[64,144,128]{2,1,0:T(8,128)(2,1)S(1)} %all_to_all.11.recv_ref, f32[512,1]{1,0:T(8,128)S(1)} %get-tuple-element.6.place_ref), custom_call_target="tpu_custom_call" | custom-call | tf_op jit(solution)/shard_map/unpack/pallas_call | solution.py:214
Async XLA Ops:
  3.4 72.9 %copy-start = (bf16[1,512,2048]{2,1,0:T(8,128)(2,1)S(1)}, bf16[1,512,2048]{2,1,0:T(8,128)(2,1)}, u32[]{:S(2)}) copy-start(bf16[1,512,2048]{2,1,0:T(8,128)(2,1)} %param.12) | copy-start | bytes 6291460
  3.4 72.9 %copy-start.1 = (bf16[1,2048,512]{2,1,0:T(8,128)(2,1)S(1)}, bf16[1,2048,512]{2,1,0:T(8,128)(2,1)}, u32[]{:S(2)}) copy-start(bf16[1,2048,512]{2,1,0:T(8,128)(2,1)} %param.13) | copy-start | bytes 6291460

commit v5 on v4

--- a/solution.py
+++ b/solution.py
@@ -11,6 +11,7 @@
 US = 32
 REQ_DEV = 8
 LANES = 128
+CORES = 2
 MIB = 1024 * 1024
 
 
@@ -72,13 +73,17 @@
     local_req = (req_ref[...] & (REQ_DEV - 1)).astype(jnp.float32)
     at_slot = iota((count, LANES), 1).astype(jnp.float32) == as_column(slot)
     requests = dot(named, jnp.where(at_slot, as_column(local_req), 0.0).astype(jnp.bfloat16))
-    user = jnp.concatenate([user_ref[:, c * LANES : (c + 1) * LANES] for c in range(chunks)], axis=0)
     tail = send_ref.shape[1] - first
-    user_tail = jnp.concatenate(
-        [user.astype(jnp.float32), jnp.zeros((tail - chunks * own, LANES), jnp.float32)], axis=0
-    )
-    is_request = iota((experts, tail, LANES), 1) == chunks * own
-    send_ref[:, first:, :] = jnp.where(is_request, requests[:, None, :], user_tail[None]).astype(jnp.bfloat16)
+    half = own // CORES
+    tails = []
+    for k in range(CORES):
+        part = [user_ref[k * half : (k + 1) * half, c * LANES : (c + 1) * LANES] for c in range(chunks)]
+        rest = jnp.zeros((tail - chunks * half, LANES), jnp.float32)
+        tails.append(jnp.concatenate([p.astype(jnp.float32) for p in part] + [rest], axis=0))
+    second = iota((experts, tail, LANES), 0) % CORES == 1
+    user_tail = jnp.where(second, tails[1][None], tails[0][None])
+    is_request = iota((experts, tail, LANES), 1) == chunks * half
+    send_ref[:, first:, :] = jnp.where(is_request, requests[:, None, :], user_tail).astype(jnp.bfloat16)
     copies[3].wait()
     copies[4].wait()
     spread = (iota((experts * capacity, count), 0).astype(jnp.float32) == place).astype(jnp.bfloat16)
@@ -86,27 +91,47 @@
     write_rows(send_ref, chunks * capacity, capacity, dot(spread, grad_ref[...]).astype(jnp.bfloat16))
 
 
-def work_kernel(capacity, own, recv_ref, w_in_ref, w_out_ref, send_ref):
+def back_kernel(capacity, recv_ref, w_out_ref, back_ref, *half_ref):
+    count = back_ref.shape[0]
+    width = w_out_ref.shape[1]
+    chunks = width // LANES
+    start = 0 if half_ref else recv_ref.shape[0] - count // capacity
+    if half_ref:
+        first = 2 * chunks * capacity
+        half_ref[0][...] = recv_ref[:, first : first + half_ref[0].shape[1], :]
+    part = recv_ref.at[start : start + count // capacity]
+    back_ref[...] = dot(read_rows(part, chunks * capacity, capacity, width), w_out_ref[...], ((1,), (1,)))
+
+
+def work_kernel(capacity, own, recv_ref, other_ref, back1_ref, back2_ref, w_in_ref, w_out_ref, send_ref):
     sources = recv_ref.shape[0]
     width = w_in_ref.shape[0]
     chunks = width // LANES
     count = sources * capacity
     scale = 1.0 / math.sqrt(width)
     emb = read_rows(recv_ref, 0, capacity, width)
-    grad = read_rows(recv_ref, chunks * capacity, capacity, width)
     first = 2 * chunks * capacity
     keys_n = sources * own
+    half = own // CORES
     user_rows = chunks * own
-    users = recv_ref[:, first : first + user_rows, :].astype(jnp.float32)
+    here = recv_ref[:, first : first + chunks * half, :].astype(jnp.float32)
+    there = other_ref[...].astype(jnp.float32)
+    low = lax.axis_index("cand") % CORES == 0
     keys = jnp.concatenate(
-        [users[:, c * own : (c + 1) * own, :].reshape(keys_n, LANES) for c in range(chunks)], axis=1
+        [
+            jnp.concatenate(
+                [rows[:, c * half : (c + 1) * half, :].reshape(sources * half, LANES) for c in range(chunks)], axis=1
+            )
+            for rows in (jnp.where(low, here, there), jnp.where(low, there, here))
+        ],
+        axis=0,
     ).astype(jnp.bfloat16)
-    requests = recv_ref[:, first + user_rows, :].astype(jnp.bfloat16)
+    requests = recv_ref[:, first + chunks * half, :].astype(jnp.bfloat16)
     source_of = (iota((count, sources), 0) // capacity == iota((count, sources), 1)).astype(jnp.bfloat16)
     spread = dot(source_of, requests)
     mine = iota((count, LANES), 1) == iota((count, LANES), 0) % capacity
     request = jnp.sum(jnp.where(mine, spread, 0.0), axis=1, keepdims=True)
-    member = (iota((count, keys_n), 1) // US).astype(jnp.float32) == request
+    member = (iota((count, keys_n), 1) % (keys_n // CORES) // (US // CORES)).astype(jnp.float32) == request
 
     scores = dot(emb, keys, ((1,), (1,))) * scale
     peak = jnp.max(jnp.where(member, scores, -jnp.inf), axis=1, keepdims=True)
@@ -120,11 +145,12 @@
     tile = count // 4
     for m in range(0, count, tile):
         pre = dot(inputs[m : m + tile], w_in_ref[...])
-        back = dot(grad[m : m + tile], w_out_ref[...], ((1,), (1,)))
+        back_ref, at = (back1_ref, m) if m < count // 2 else (back2_ref, m - count // 2)
+        back = back_ref[at : at + tile, :]
         square = pre * pre
-        half = 0.5 + 0.5 * jnp.tanh(pre * (c0 + (c0 * 0.044715) * square))
-        gelu = pre * half
-        slope_g = half + gelu * (1.0 - half) * (2.0 * c0 + (6.0 * c0 * 0.044715) * square)
+        upper = 0.5 + 0.5 * jnp.tanh(pre * (c0 + (c0 * 0.044715) * square))
+        gelu = pre * upper
+        slope_g = upper + gelu * (1.0 - upper) * (2.0 * c0 + (6.0 * c0 * 0.044715) * square)
         outs.append(dot(gelu.astype(jnp.bfloat16), w_out_ref[...]).astype(jnp.bfloat16))
         backs.append(dot((back * slope_g).astype(jnp.bfloat16), w_in_ref[...], ((1,), (1,))).astype(jnp.bfloat16))
     write_rows(send_ref, 0, capacity, jnp.concatenate(outs, axis=0))
@@ -136,8 +162,14 @@
     cand_grad = d_in.astype(jnp.float32) + dot(slope, keys) * scale
     write_rows(send_ref, chunks * capacity, capacity, cand_grad.astype(jnp.bfloat16))
     share = dot(probs_b, d_in, ((0,), (0,))) + dot(slope, emb, ((0,), (0,))) * scale
+    part = keys_n // CORES
     tail = jnp.concatenate(
-        [share[:, c * LANES : (c + 1) * LANES].reshape(sources, own, LANES) for c in range(chunks)], axis=1
+        [
+            share[k * part : (k + 1) * part, c * LANES : (c + 1) * LANES].reshape(sources, half, LANES)
+            for c in range(chunks)
+            for k in range(CORES)
+        ],
+        axis=1,
     )
     send_ref[:, first : first + user_rows, :] = tail.astype(jnp.bfloat16)
 
@@ -153,16 +185,14 @@
     copies = [pltpu.make_async_copy(user_ref, user_hbm, sems.at[0])]
     copies[0].start()
     pick = (iota((count, experts * capacity), 1).astype(jnp.float32) == place_ref[...]).astype(jnp.bfloat16)
-    out_ref[...] = dot(pick, read_rows(recv_ref, 0, capacity, width)).astype(jnp.bfloat16)
-    copies.append(pltpu.make_async_copy(out_ref, out_hbm, sems.at[1]))
-    copies[1].start()
-    grads = read_rows(recv_ref, chunks * capacity, capacity, width)
-    part = count // 2
-    for p in range(2):
-        rows = pl.ds(p * part, part)
-        grad_ref[rows, :] = dot(pick[p * part : (p + 1) * part], grads).astype(jnp.bfloat16)
-        copies.append(pltpu.make_async_copy(grad_ref.at[rows, :], grad_hbm.at[rows, :], sems.at[2 + p]))
-        copies[2 + p].start()
+    part = count // 4
+    for first_row, to_ref, to_hbm in ((0, out_ref, out_hbm), (chunks * capacity, grad_ref, grad_hbm)):
+        values = read_rows(recv_ref, first_row, capacity, width)
+        for p in range(4):
+            rows = pl.ds(p * part, part)
+            to_ref[rows, :] = dot(pick[p * part : (p + 1) * part], values).astype(jnp.bfloat16)
+            copies.append(pltpu.make_async_copy(to_ref.at[rows, :], to_hbm.at[rows, :], sems.at[len(copies)]))
+            copies[-1].start()
     for copy in copies:
         copy.wait()
 
@@ -178,7 +208,7 @@
     capacity = 2 * count // experts
     chunks = width // LANES
     body = chunks * (2 * capacity + own)
-    there = body + 8
+    there = 2 * chunks * capacity + 16
     hbm = pl.BlockSpec(memory_space=pltpu.HBM)
     send, place = pl.pallas_call(
         functools.partial(pack_kernel, capacity),
@@ -199,12 +229,29 @@
         name="pack",
     )(expert_ids[None], cand_req[None], cand_emb, d_out, user_state)
     recv = exchange(send)
+    slots = experts * capacity
+    back_flops = slots * width * w_in.shape[2]
+    half_rows = chunks * own // CORES
+
+    def back(outs):
+        return pl.pallas_call(
+            functools.partial(back_kernel, capacity),
+            out_shape=outs,
+            compiler_params=pltpu.CompilerParams(vmem_limit_bytes=24 * MIB),
+            cost_estimate=pl.CostEstimate(flops=back_flops, bytes_accessed=8 * MIB, transcendentals=0),
+            name="back",
+        )(recv, w_out[0])
+
+    products = pltpu.VMEM((slots // 2, w_in.shape[2]), jnp.float32)
+    back1, half = back((products, jax.ShapeDtypeStruct((experts, half_rows, LANES), jnp.bfloat16)))
+    other = lax.ppermute(half, "cand", [(i, i ^ 1) for i in range(experts)])
+    (back2,) = back((products,))
     send = pl.pallas_call(
         functools.partial(work_kernel, capacity, own),
         out_shape=jax.ShapeDtypeStruct((experts, body, LANES), jnp.bfloat16),
         compiler_params=pltpu.CompilerParams(vmem_limit_bytes=30 * MIB),
         name="work",
-    )(recv, w_in[0], w_out[0])
+    )(recv, other, back1, back2, w_in[0], w_out[0])
     recv = exchange(send)
     outs = (
         jax.ShapeDtypeStruct((count, width), jnp.bfloat16),
@@ -215,7 +262,7 @@
         functools.partial(unpack_kernel, capacity, own),
         out_shape=outs,
         out_specs=(hbm, hbm, hbm),
-        scratch_shapes=[pltpu.VMEM(o.shape, o.dtype) for o in outs] + [pltpu.SemaphoreType.DMA((4,))],
+        scratch_shapes=[pltpu.VMEM(o.shape, o.dtype) for o in outs] + [pltpu.SemaphoreType.DMA((9,))],
         compiler_params=pltpu.CompilerParams(vmem_limit_bytes=24 * MIB),
         name="unpack",
     )(recv, place)

time: 154 us -> 153 us (level)
  blocking collectives: 136 us -> 133 us
    all_to_all x2, blocking collectives: 136 us -> 133 us  [exchange(): lax.all_to_all(blocks, 'cand', split_axis=0, concat_axis=0, tiled=True)]
    pallas_call x0 -> x2, Pallas kernels: none -> 2.56 us  [back(): pl.pallas_call(functools.partial(back_kernel, capacity), out_shape=outs,...]
  transfers between devices with their start and end apart: 0 -> 1, of which waited for: 0 -> 0; matrix products, arithmetic and copies ran while one was open for 0% -> 0% of each run, Pallas kernels for 0% -> 1%
where the time goes in v5:
time: 153 us; the launch traced here: 152 us
  blocking collectives  133 us (87%)
  Pallas kernels  18.4 us (12%)
    all_to_all x2, blocking collectives, exchange(): lax.all_to_all(blocks, 'cand', split_axis=0, concat_axis=0, tiled=True)  133 us
    pallas_call x1, Pallas kernels, shards(): pl.pallas_call(functools.partial(work_kernel, capacity, own), out_shape=j...  11 us
  transfers between devices with their start and end apart: 1, of which 0 were waited for; matrix products, arithmetic and copies ran while one was open for 0% of the time, Pallas kernels for 1%

profile of v5, /device:TPU:1, one launch (start us, length us, event | category | flops | bytes accessed | tf_op | source)
XLA Modules:
  0.0 152.4 jit_solution(2253033083907408498)
XLA Ops:
  0.6 2.7 %pack.1 = (bf16[64,144,128]{2,1,0:T(8,128)(2,1)S(1)}, f32[512,1]{1,0:T(8,128)S(1)}) custom-call(s32[1,512]{1,0:T(1,128)} %bitcast.8, s32[1,512]{1,0:T(1,128)} %bitcast.9, bf16[512,512]{1,0:T(8,128)(2,1)} %emb_hbm.1, bf16[512,512]{1,0:T(8,128)(2,1)} %grad_hbm.1, bf16[4,512]{1,0:T(4,128)(2,1)} %user_hbm.1), custom_call_target="tpu_custom_call" | custom-call | tf_op jit(solution)/shard_map/pack/pallas_call | solution.py:213
  3.4 0.0 copy-start
  3.4 70.0 %all_to_all.10.recv_ref = bf16[64,144,128]{2,1,0:T(8,128)(2,1)S(1)} all-to-all(bf16[64,144,128]{2,1,0:T(8,128)(2,1)S(1)} %get-tuple-element.7), channel_id=1, replica_groups=mesh['req'=4,'cand'=64] {'cand'}, dimensions={0} | all-to-all | bytes 4718592 | tf_op jit(solution)/shard_map/all_to_all | solution.py:201
  73.4 0.0 copy-done
  73.4 1.3 back.2
  74.7 0.0 copy-start.1
  74.7 0.7 collective-permute-start
  75.4 1.3 back.3.back2_ref
  76.7 0.0 collective-permute-done.other_ref
  76.7 0.0 copy-done.1
  76.7 11.0 %work.1 = bf16[64,144,128]{2,1,0:T(8,128)(2,1)S(1)} custom-call(bf16[64,144,128]{2,1,0:T(8,128)(2,1)S(1)} %all_to_all.10.recv_ref, bf16[64,8,128]{2,1,0:T(8,128)(2,1)S(1)} %collective-permute-done.other_ref, f32[512,2048]{1,0:T(8,128)S(1)} %get-tuple-element.9.back1_ref, f32[512,2048]{1,0:T(8,128)S(1)} %back.3.back2_ref, bf16[512,2048]{1,0:T(8,128)(2,1)S(1)} %bitcast.7, ...), custom_call_target="tpu_custom_call" | custom-call | tf_op jit(solution)/shard_map/work/pallas_call | solution.py:249
  87.7 62.5 %all_to_all.11.recv_ref = bf16[64,144,128]{2,1,0:T(8,128)(2,1)S(1)} all-to-all(bf16[64,144,128]{2,1,0:T(8,128)(2,1)S(1)} %work.1), channel_id=1, replica_groups=mesh['req'=4,'cand'=64] {'cand'}, dimensions={0} | all-to-all | bytes 4718592 | tf_op jit(solution)/shard_map/all_to_all | solution.py:201
  150.2 2.0 %unpack.1 = (bf16[512,512]{1,0:T(8,128)(2,1)}, bf16[512,512]{1,0:T(8,128)(2,1)}, f32[4,512]{1,0:T(4,128)}) custom-call(bf16[64,144,128]{2,1,0:T(8,128)(2,1)S(1)} %all_to_all.11.recv_ref, f32[512,1]{1,0:T(8,128)S(1)} %get-tuple-element.10.place_ref), custom_call_target="tpu_custom_call" | custom-call | tf_op jit(solution)/shard_map/unpack/pallas_call | solution.py:261
Async XLA Ops:
  3.4 70.0 %copy-start = (bf16[1,2048,512]{2,1,0:T(8,128)(2,1)S(1)}, bf16[1,2048,512]{2,1,0:T(8,128)(2,1)}, u32[]{:S(2)}) copy-start(bf16[1,2048,512]{2,1,0:T(8,128)(2,1)} %param.13) | copy-start | bytes 6291460
  74.7 2.0 %copy-start.1 = (bf16[1,512,2048]{2,1,0:T(8,128)(2,1)S(1)}, bf16[1,512,2048]{2,1,0:T(8,128)(2,1)}, u32[]{:S(2)}) copy-start(bf16[1,512,2048]{2,1,0:T(8,128)(2,1)} %param.12) | copy-start | bytes 6291460
  74.7 2.0 %collective-permute-start = (bf16[64,8,128]{2,1,0:T(8,128)(2,1)S(1)}, bf16[64,8,128]{2,1,0:T(8,128)(2,1)S(1)}, u32[]{:S(2)}, u32[]{:S(2)}) collective-permute-start(bf16[64,8,128]{2,1,0:T(8,128)(2,1)S(1)} %get-tuple-element.8), channel_id=1, source_target_pairs={{0,1},{1,0},{2,3},{3,2},{4,5},{5,4},{6,7},{7,6},{8,9},{9,8},{10,11... | collective-permute-start | bytes 393224 | tf_op jit(solution)/shard_map/ppermute | solution.py:247

commit v6 on v5

--- a/solution.py
+++ b/solution.py
@@ -95,7 +95,7 @@
     count = back_ref.shape[0]
     width = w_out_ref.shape[1]
     chunks = width // LANES
-    start = 0 if half_ref else recv_ref.shape[0] - count // capacity
+    start = 0 if half_ref else recv_ref.shape[0] // 4
     if half_ref:
         first = 2 * chunks * capacity
         half_ref[0][...] = recv_ref[:, first : first + half_ref[0].shape[1], :]
@@ -110,6 +110,8 @@
     count = sources * capacity
     scale = 1.0 / math.sqrt(width)
     emb = read_rows(recv_ref, 0, capacity, width)
+    last = recv_ref.at[sources - sources // 4 :]
+    grad = read_rows(last, chunks * capacity, capacity, width)
     first = 2 * chunks * capacity
     keys_n = sources * own
     half = own // CORES
@@ -145,8 +147,12 @@
     tile = count // 4
     for m in range(0, count, tile):
         pre = dot(inputs[m : m + tile], w_in_ref[...])
-        back_ref, at = (back1_ref, m) if m < count // 2 else (back2_ref, m - count // 2)
-        back = back_ref[at : at + tile, :]
+        if m < tile:
+            back = back1_ref[...]
+        elif m < 3 * tile:
+            back = back2_ref[m - tile : m, :]
+        else:
+            back = dot(grad, w_out_ref[...], ((1,), (1,)))
         square = pre * pre
         upper = 0.5 + 0.5 * jnp.tanh(pre * (c0 + (c0 * 0.044715) * square))
         gelu = pre * upper
@@ -242,10 +248,9 @@
             name="back",
         )(recv, w_out[0])
 
-    products = pltpu.VMEM((slots // 2, w_in.shape[2]), jnp.float32)
-    back1, half = back((products, jax.ShapeDtypeStruct((experts, half_rows, LANES), jnp.bfloat16)))
+    back1, half = back((pltpu.VMEM((slots // 4, w_in.shape[2]), jnp.float32), jax.ShapeDtypeStruct((experts, half_rows, LANES), jnp.bfloat16)))
     other = lax.ppermute(half, "cand", [(i, i ^ 1) for i in range(experts)])
-    (back2,) = back((products,))
+    (back2,) = back((pltpu.VMEM((slots // 2, w_in.shape[2]), jnp.float32),))
     send = pl.pallas_call(
         functools.partial(work_kernel, capacity, own),
         out_shape=jax.ShapeDtypeStruct((experts, body, LANES), jnp.bfloat16),

time: 153 us -> 152 us (level)
  no operation moved by 1% of the time
where the time goes in v6:
time: 152 us
  blocking collectives  133 us (88%)
  Pallas kernels  18.1 us (12%)
    all_to_all x2, blocking collectives, exchange(): lax.all_to_all(blocks, 'cand', split_axis=0, concat_axis=0, tiled=True)  133 us
    pallas_call x1, Pallas kernels, shards(): pl.pallas_call(functools.partial(work_kernel, capacity, own), out_shape=j...  11.3 us
  transfers between devices with their start and end apart: 1, of which 0 were waited for; matrix products, arithmetic and copies ran while one was open for 0% of the time, Pallas kernels for 1%

profile of v6, /device:TPU:1, one launch (start us, length us, event | category | flops | bytes accessed | tf_op | source)
XLA Modules:
  0.0 152.2 jit_solution(16310235667763788305)
XLA Ops:
  0.6 2.7 %pack.1 = (bf16[64,144,128]{2,1,0:T(8,128)(2,1)S(1)}, f32[512,1]{1,0:T(8,128)S(1)}) custom-call(s32[1,512]{1,0:T(1,128)} %bitcast.8, s32[1,512]{1,0:T(1,128)} %bitcast.9, bf16[512,512]{1,0:T(8,128)(2,1)} %emb_hbm.1, bf16[512,512]{1,0:T(8,128)(2,1)} %grad_hbm.1, bf16[4,512]{1,0:T(4,128)(2,1)} %user_hbm.1), custom_call_target="tpu_custom_call" | custom-call | tf_op jit(solution)/shard_map/pack/pallas_call | solution.py:219
  3.4 0.0 copy-start
  3.4 70.0 %all_to_all.10.recv_ref = bf16[64,144,128]{2,1,0:T(8,128)(2,1)S(1)} all-to-all(bf16[64,144,128]{2,1,0:T(8,128)(2,1)S(1)} %get-tuple-element.7), channel_id=1, replica_groups=mesh['req'=4,'cand'=64] {'cand'}, dimensions={0} | all-to-all | bytes 4718592 | tf_op jit(solution)/shard_map/all_to_all | solution.py:207
  73.4 0.0 copy-done
  73.4 0.7 back.2
  74.2 0.0 copy-start.1
  74.2 0.7 collective-permute-start
  74.8 1.3 back.3.back2_ref
  76.1 0.0 collective-permute-done.other_ref
  76.1 0.0 copy-done.1
  76.1 11.3 %work.1 = bf16[64,144,128]{2,1,0:T(8,128)(2,1)S(1)} custom-call(bf16[64,144,128]{2,1,0:T(8,128)(2,1)S(1)} %all_to_all.10.recv_ref, bf16[64,8,128]{2,1,0:T(8,128)(2,1)S(1)} %collective-permute-done.other_ref, f32[256,2048]{1,0:T(8,128)S(1)} %get-tuple-element.9.back1_ref, f32[512,2048]{1,0:T(8,128)S(1)} %back.3.back2_ref, bf16[512,2048]{1,0:T(8,128)(2,1)S(1)} %bitcast.7, ...), custom_call_target="tpu_custom_call" | custom-call | tf_op jit(solution)/shard_map/work/pallas_call | solution.py:254
  87.5 62.5 %all_to_all.11.recv_ref = bf16[64,144,128]{2,1,0:T(8,128)(2,1)S(1)} all-to-all(bf16[64,144,128]{2,1,0:T(8,128)(2,1)S(1)} %work.1), channel_id=1, replica_groups=mesh['req'=4,'cand'=64] {'cand'}, dimensions={0} | all-to-all | bytes 4718592 | tf_op jit(solution)/shard_map/all_to_all | solution.py:207
  150.0 2.0 %unpack.1 = (bf16[512,512]{1,0:T(8,128)(2,1)}, bf16[512,512]{1,0:T(8,128)(2,1)}, f32[4,512]{1,0:T(4,128)}) custom-call(bf16[64,144,128]{2,1,0:T(8,128)(2,1)S(1)} %all_to_all.11.recv_ref, f32[512,1]{1,0:T(8,128)S(1)} %get-tuple-element.10.place_ref), custom_call_target="tpu_custom_call" | custom-call | tf_op jit(solution)/shard_map/unpack/pallas_call | solution.py:266
Async XLA Ops:
  3.4 70.0 %copy-start = (bf16[1,2048,512]{2,1,0:T(8,128)(2,1)S(1)}, bf16[1,2048,512]{2,1,0:T(8,128)(2,1)}, u32[]{:S(2)}) copy-start(bf16[1,2048,512]{2,1,0:T(8,128)(2,1)} %param.13) | copy-start | bytes 6291460
  74.2 2.0 %copy-start.1 = (bf16[1,512,2048]{2,1,0:T(8,128)(2,1)S(1)}, bf16[1,512,2048]{2,1,0:T(8,128)(2,1)}, u32[]{:S(2)}) copy-start(bf16[1,512,2048]{2,1,0:T(8,128)(2,1)} %param.12) | copy-start | bytes 6291460
  74.2 2.0 %collective-permute-start = (bf16[64,8,128]{2,1,0:T(8,128)(2,1)S(1)}, bf16[64,8,128]{2,1,0:T(8,128)(2,1)S(1)}, u32[]{:S(2)}, u32[]{:S(2)}) collective-permute-start(bf16[64,8,128]{2,1,0:T(8,128)(2,1)S(1)} %get-tuple-element.8), channel_id=1, source_target_pairs={{0,1},{1,0},{2,3},{3,2},{4,5},{5,4},{6,7},{7,6},{8,9},{9,8},{10,11... | collective-permute-start | bytes 393224 | tf_op jit(solution)/shard_map/ppermute | solution.py:252
